TPU v7x, 1024 devices: a whole 4x4x32 slice. The times are simulated.
1024 devices in a mesh: dp: 32 (over z), ctx: 16 (over x_hi, y, core), tp: 2 (over x_lo).
Axes of the slice: x: 4 (x_hi: 2, x_lo: 2; x = x_hi * 2 + x_lo), y: 4, z: 32, core: 2. Of those that a mesh axis runs over, the one named last changes fastest.
Arguments:
- queries: bfloat16 [32, 2048, 4096], P('dp', 'ctx', 'tp'), may hold values from -8 to 8
- keys_text: bfloat16 [32, 2048, 512], P('dp', 'ctx', 'tp'), may hold values from -8 to 8
- values_text: bfloat16 [32, 2048, 512], P('dp', 'ctx', 'tp'), may hold values from -6 to 6
- patch_rows: bfloat16 [32, 16, 64, 2, 512], P('dp', 'ctx', None, None, 'tp'), may hold values from -6 to 6
- patch_owner: int32 [32, 16, 64, 1], P('dp', 'ctx'), may hold values from 0 to 31; in each aligned block of 64 rows (0 to 63, 64 to 127, ..., all dimensions but the last counted through in order) at most 4 rows name the same one
- patch_place: int32 [32, 16, 64], P('dp', 'ctx'), may hold values from 0 to 127
- value_head: bfloat16 [4096], P('tp'), may hold values from -0.75 to 0.75
Outputs:
- attention: bfloat16 [32, 2048, 4096], P('dp', 'ctx', 'tp')
- value_out: float32 [32, 2048], P('dp', 'ctx')
Inputs may be any that keep to these rules, and one draw needn't show every extreme that they name: `patch_owner`: among the rows of one vision shard at most 4 name the same sequence, and exactly 4 do in some shards. `patch_place`: rows that share an owner, a ctx index and a position are all added there.
All inputs are finite; a program needn't handle non-finite values.
Results may differ from a plain program's by a relative error of at most 0.0079.
Values may be sent and summed in bfloat16 or wider, within the bound.
No kernel may reach another device: no remote copies, remote signals or barrier semaphores. Data moves between devices by JAX's collectives and lax.ppermute only.
A program may use at most 32 MiB of HBM per device.

v0:
```python
import jax
import jax.numpy as jnp
from jax import lax
from jax.sharding import PartitionSpec as P

HD = 128
CAP = 4


def from_everyone(value, axis):
    count = lax.axis_size(axis)
    return lax.all_to_all(
        jnp.broadcast_to(value[None], (count, *value.shape)), axis, 0, 0, tiled=True
    )


def taken_together(value, axis):
    return from_everyone(value, axis).sum(axis=0)


def body(queries, keys_text, values_text, patch_rows, patch_owner, patch_place, value_head):
    token_count = queries.shape[1]
    kv_width = keys_text.shape[2]
    groups = kv_width // HD
    head_count = queries.shape[2] // HD
    group_size = head_count // groups
    score_scale = HD ** (-0.5)
    dp_count = lax.axis_size("dp")
    ctx_count = lax.axis_size("ctx")
    slot_count = dp_count * CAP
    owner_seq = patch_owner[0, 0, :, 0]
    places = patch_place[0, 0]
    owner_hits = (owner_seq[:, None] == jnp.arange(dp_count, dtype=jnp.int32)[None, :]).astype(
        jnp.int32
    )
    before = jnp.cumsum(owner_hits, axis=0) - owner_hits
    slot_rank = jnp.sum(before * owner_hits, axis=1)
    target = owner_seq * CAP + slot_rank
    select = (jnp.arange(slot_count, dtype=jnp.int32)[:, None] == target[None, :]).astype(jnp.int32)
    row_data = patch_rows[0, 0].reshape(places.shape[0], 2 * kv_width)
    packed = jnp.dot(
        select.astype(jnp.bfloat16), row_data, preferred_element_type=jnp.float32
    ).astype(jnp.bfloat16)
    filled = jnp.sum(select, axis=1)
    slot_place = jnp.sum(select * places[None, :], axis=1) + (1 - filled) * token_count
    packed = packed.reshape(slot_count, 2, kv_width)
    arrived, arrived_place = (
        lax.all_to_all(packed, "dp", split_axis=0, concat_axis=0, tiled=True),
        lax.all_to_all(slot_place, "dp", split_axis=0, concat_axis=0, tiled=True),
    )
    landing = (jnp.arange(token_count, dtype=jnp.int32)[:, None] == arrived_place[None, :]).astype(
        jnp.bfloat16
    )
    arrivals = jnp.dot(
        landing, arrived.reshape(slot_count, 2 * kv_width), preferred_element_type=jnp.float32
    )
    merged_keys = (keys_text[0].astype(jnp.float32) + arrivals[:, :kv_width]).astype(jnp.bfloat16)
    merged_values = (values_text[0].astype(jnp.float32) + arrivals[:, kv_width:]).astype(
        jnp.bfloat16
    )
    local_heads = head_count // ctx_count

    def widen(tensor):
        spread = jnp.repeat(tensor.reshape(token_count, groups, HD), group_size, axis=1)
        return spread.reshape(token_count, ctx_count, local_heads, HD)

    query_split = queries[0].reshape(token_count, ctx_count, local_heads, HD)
    head_queries = lax.all_to_all(query_split, "ctx", split_axis=1, concat_axis=0, tiled=True)
    head_keys = lax.all_to_all(widen(merged_keys), "ctx", split_axis=1, concat_axis=0, tiled=True)
    head_values = lax.all_to_all(
        widen(merged_values), "ctx", split_axis=1, concat_axis=0, tiled=True
    )
    length = head_queries.shape[0]
    block_rows = 512
    results = []
    for lower in range(0, length, block_rows):
        upper = lower + block_rows
        scores = (
            jnp.einsum(
                "thd,shd->ths",
                head_queries[lower:upper, 0],
                head_keys[:upper, 0],
                preferred_element_type=jnp.float32,
            )
            * score_scale
        )
        allowed = (
            jnp.arange(upper, dtype=jnp.int32)[None, :]
            <= (lower + jnp.arange(block_rows, dtype=jnp.int32))[:, None]
        )
        allowed = allowed[:, None, :]
        scores = jnp.where(allowed, scores, -1e30)
        row_max = jnp.max(scores, axis=-1)
        weights = jnp.where(allowed, jnp.exp(scores - row_max[..., None]), 0.0)
        denominator = jnp.sum(weights, axis=-1)
        mixed = (
            jnp.einsum(
                "ths,shd->thd",
                weights.astype(jnp.bfloat16),
                head_values[:upper, 0],
                preferred_element_type=jnp.float32,
            )
            / denominator[..., None]
        )
        results.append(mixed.astype(jnp.bfloat16))
    joined = jnp.concatenate(results, axis=0)[:, None]
    gathered = lax.all_to_all(joined, "ctx", split_axis=0, concat_axis=1, tiled=True)
    attention = gathered.reshape(token_count, head_count * HD)
    partial_value = jnp.dot(attention, value_head, preferred_element_type=jnp.float32)
    value_out = taken_together(partial_value, "tp")
    return (attention[None], value_out[None])


def solution(mesh):
    in_specs = (
        P("dp", "ctx", "tp"),
        P("dp", "ctx", "tp"),
        P("dp", "ctx", "tp"),
        P("dp", "ctx", None, None, "tp"),
        P("dp", "ctx", None, None),
        P("dp", "ctx", None),
        P("tp"),
    )
    out_specs = (P("dp", "ctx", "tp"), P("dp", "ctx"))
    return jax.shard_map(body, mesh=mesh, in_specs=in_specs, out_specs=out_specs, check_vma=False)
```

profile of v0, /device:TPU:1, one launch (start us, length us, event | category | flops | bytes accessed | tf_op | source)
XLA Modules:
  0.0 176.2 jit_solution(2943183616569429626)
XLA Ops:
  0.6 0.8 fusion.62
  1.5 0.8 select_reduce_fusion.1
  4.5 29.3 %all-to-all-start = ((s32[32,4,1]{1,2,0:T(1,128)}), s32[32,4,1]{1,2,0:T(1,128)S(1)}, u32[]{:S(2)}, u32[]{:S(2)}) async-start(s32[32,4,1]{1,2,0:T(1,128)} %bitcast.3), calls=%async_computation | async-start | bytes 32768 | tf_op jit(solution)/shard_map/all_to_all | solution.py:49
  33.8 0.9 copy.73
  35.6 19.4 %all-to-all-done = s32[32,4,1]{1,2,0:T(1,128)S(1)} async-done(((s32[32,4,1]{1,2,0:T(1,128)}), s32[32,4,1]{1,2,0:T(1,128)S(1)}, u32[]{:S(2)}, u32[]{:S(2)}) %all-to-all-start) | async-done | bytes 544 | tf_op jit(solution)/shard_map/all_to_all | solution.py:49
  55.0 3.9 %all-to-all-start.1 = ((bf16[128,2,256]{2,1,0:T(2,128)(2,1)}), bf16[128,2,256]{2,1,0:T(2,128)(2,1)S(1)}, u32[]{:S(2)}, u32[]{:S(2)}) async-start(bf16[128,2,256]{2,1,0:T(2,128)(2,1)} %reshape.319), calls=%async_computation.1 | async-start | bytes 262144 | tf_op jit(solution)/shard_map/all_to_all | solution.py:48
  58.8 2.0 %copy.62 = bf16[1,128,2048]{1,2,0:T(8,128)(2,1)} copy(bf16[1,128,2048]{2,1,0:T(8,128)(2,1)} %param.7) | data formatting | bytes 1048576 | tf_op args[0]
  62.2 23.7 %all-to-all-done.1 = bf16[128,2,256]{2,1,0:T(2,128)(2,1)S(1)} async-done(((bf16[128,2,256]{2,1,0:T(2,128)(2,1)}), bf16[128,2,256]{2,1,0:T(2,128)(2,1)S(1)}, u32[]{:S(2)}, u32[]{:S(2)}) %all-to-all-start.1) | async-done | bytes 131104 | tf_op jit(solution)/shard_map/all_to_all | solution.py:48
  85.9 12.4 %all-to-all-start.4 = ((bf16[128,16,1,128]{0,3,2,1:T(8,128)(2,1)}), bf16[128,16,1,128]{0,3,2,1:T(8,128)(2,1)S(1)}, u32[]{:S(2)}, u32[]{:S(2)}) async-start(bf16[128,16,1,128]{0,3,2,1:T(8,128)(2,1)} %bitcast.14), calls=%async_computation.4 | async-start | bytes 1048576 | tf_op jit(solution)/shard_map/all_to_all | solution.py:68
  98.6 11.0 %all-to-all-done.4 = bf16[128,16,1,128]{0,3,2,1:T(8,128)(2,1)S(1)} async-done(((bf16[128,16,1,128]{0,3,2,1:T(8,128)(2,1)}), bf16[128,16,1,128]{0,3,2,1:T(8,128)(2,1)S(1)}, u32[]{:S(2)}, u32[]{:S(2)}) %all-to-all-start.4) | async-done | bytes 524320 | tf_op jit(solution)/shard_map/all_to_all | solution.py:68
  109.7 15.0 %all_to_all.77 = bf16[128,16,1,128]{3,0,2,1:T(8,128)(2,1)S(1)} all-to-all(bf16[128,16,1,128]{3,0,2,1:T(8,128)(2,1)S(1)} %bitcast.209), channel_id=1, replica_groups=mesh['dp'=32,'ctx'=16,'tp'=2] {'ctx'}, dimensions={1} | all-to-all | bytes 1048576 | tf_op jit(solution)/shard_map/all_to_all | solution.py:69
  124.7 0.9 broadcast_in_dim.38
  125.5 4.5 %all-to-all-start.2 = ((bf16[128,16,1,128]{3,0,2,1:T(8,128)(2,1)}), bf16[128,16,1,128]{3,0,2,1:T(8,128)(2,1)S(1)}, u32[]{:S(2)}, u32[]{:S(2)}) async-start(bf16[128,16,1,128]{3,0,2,1:T(8,128)(2,1)} %bitcast.4), calls=%async_computation.2 | async-start | bytes 1048576 | tf_op jit(solution)/shard_map/all_to_all | solution.py:70
  130.5 11.0 %all-to-all-done.2 = bf16[128,16,1,128]{3,0,2,1:T(8,128)(2,1)S(1)} async-done(((bf16[128,16,1,128]{3,0,2,1:T(8,128)(2,1)}), bf16[128,16,1,128]{3,0,2,1:T(8,128)(2,1)S(1)}, u32[]{:S(2)}, u32[]{:S(2)}) %all-to-all-start.2) | async-done | bytes 524320 | tf_op jit(solution)/shard_map/all_to_all | solution.py:70
  146.2 0.8 fusion
  147.0 1.2 fusion.3
  148.2 1.2 fusion.36
  150.1 1.0 reduce.13
  151.4 0.9 reshape.353
  152.3 4.5 %all-to-all-start.5 = ((bf16[16,2,8192]{2,1,0:T(2,128)(2,1)}), bf16[16,2,8192]{2,1,0:T(2,128)(2,1)S(1)}, u32[]{:S(2)}, u32[]{:S(2)}) async-start(bf16[16,2,8192]{2,1,0:T(2,128)(2,1)} %reshape.353), calls=%async_computation.5 | async-start | bytes 1048576 | tf_op jit(solution)/shard_map/all_to_all | solution.py:107
  156.8 11.4 %all-to-all-done.5 = bf16[16,2,8192]{2,1,0:T(2,128)(2,1)S(1)} async-done(((bf16[16,2,8192]{2,1,0:T(2,128)(2,1)}), bf16[16,2,8192]{2,1,0:T(2,128)(2,1)S(1)}, u32[]{:S(2)}, u32[]{:S(2)}) %all-to-all-start.5) | async-done | bytes 524320 | tf_op jit(solution)/shard_map/all_to_all | solution.py:107
  169.9 3.2 %all-to-all-start.6 = ((f32[2,1,128]{2,1,0:T(1,128)}), f32[2,1,128]{2,1,0:T(1,128)S(1)}, u32[]{:S(2)}, u32[]{:S(2)}) async-start(f32[2,1,128]{2,1,0:T(1,128)} %broadcast_in_dim.82), calls=%async_computation.6 | async-start | bytes 2048 | tf_op jit(solution)/shard_map/all_to_all | solution.py:12
  173.1 1.0 copy.69
  174.1 1.6 all-to-all-done.6
  (51 shorter events, 13.0 us)
Async XLA Ops:
  0.6 97.8 %copy-start = (bf16[1,128,256]{2,1,0:T(8,128)(2,1)S(1)}, bf16[1,128,256]{2,1,0:T(8,128)(2,1)}, u32[]{:S(2)}) copy-start(bf16[1,128,256]{2,1,0:T(8,128)(2,1)} %param.8) | copy-start | bytes 196612
  0.6 97.8 %copy-start.1 = (bf16[1,128,256]{2,1,0:T(8,128)(2,1)S(1)}, bf16[1,128,256]{2,1,0:T(8,128)(2,1)}, u32[]{:S(2)}) copy-start(bf16[1,128,256]{2,1,0:T(8,128)(2,1)} %param.9) | copy-start | bytes 196612
  4.5 50.5 %all-to-all-start = ((s32[32,4,1]{1,2,0:T(1,128)}), s32[32,4,1]{1,2,0:T(1,128)S(1)}, u32[]{:S(2)}, u32[]{:S(2)}) async-start(s32[32,4,1]{1,2,0:T(1,128)} %bitcast.3), calls=%async_computation | async-start | bytes 32768 | tf_op jit(solution)/shard_map/all_to_all | solution.py:49
  55.0 31.0 %all-to-all-start.1 = ((bf16[128,2,256]{2,1,0:T(2,128)(2,1)}), bf16[128,2,256]{2,1,0:T(2,128)(2,1)S(1)}, u32[]{:S(2)}, u32[]{:S(2)}) async-start(bf16[128,2,256]{2,1,0:T(2,128)(2,1)} %reshape.319), calls=%async_computation.1 | async-start | bytes 262144 | tf_op jit(solution)/shard_map/all_to_all | solution.py:48
  85.9 23.6 %all-to-all-start.4 = ((bf16[128,16,1,128]{0,3,2,1:T(8,128)(2,1)}), bf16[128,16,1,128]{0,3,2,1:T(8,128)(2,1)S(1)}, u32[]{:S(2)}, u32[]{:S(2)}) async-start(bf16[128,16,1,128]{0,3,2,1:T(8,128)(2,1)} %bitcast.14), calls=%async_computation.4 | async-start | bytes 1048576 | tf_op jit(solution)/shard_map/all_to_all | solution.py:68
  125.5 15.9 %all-to-all-start.2 = ((bf16[128,16,1,128]{3,0,2,1:T(8,128)(2,1)}), bf16[128,16,1,128]{3,0,2,1:T(8,128)(2,1)S(1)}, u32[]{:S(2)}, u32[]{:S(2)}) async-start(bf16[128,16,1,128]{3,0,2,1:T(8,128)(2,1)} %bitcast.4), calls=%async_computation.2 | async-start | bytes 1048576 | tf_op jit(solution)/shard_map/all_to_all | solution.py:70
  149.5 7.3 %copy-start.2 = (bf16[2048]{0:T(1024)(128)(2,1)S(1)}, bf16[2048]{0:T(1024)(128)(2,1)}, u32[]{:S(2)}) copy-start(bf16[2048]{0:T(1024)(128)(2,1)} %param.13) | copy-start | bytes 12292
  152.3 15.9 %all-to-all-start.5 = ((bf16[16,2,8192]{2,1,0:T(2,128)(2,1)}), bf16[16,2,8192]{2,1,0:T(2,128)(2,1)S(1)}, u32[]{:S(2)}, u32[]{:S(2)}) async-start(bf16[16,2,8192]{2,1,0:T(2,128)(2,1)} %reshape.353), calls=%async_computation.5 | async-start | bytes 1048576 | tf_op jit(solution)/shard_map/all_to_all | solution.py:107
  169.9 5.8 %all-to-all-start.6 = ((f32[2,1,128]{2,1,0:T(1,128)}), f32[2,1,128]{2,1,0:T(1,128)S(1)}, u32[]{:S(2)}, u32[]{:S(2)}) async-start(f32[2,1,128]{2,1,0:T(1,128)} %broadcast_in_dim.82), calls=%async_computation.6 | async-start | bytes 2048 | tf_op jit(solution)/shard_map/all_to_all | solution.py:12
where the time goes:
time: 177 us; the launch traced here: 176 us
  waiting for transfers between devices  78 us (44%)
  starting transfers between devices  57.8 us (33%)
  blocking collectives  15 us (8%)
  local copies, waits for them, and re-layouts  10.6 us (6%)
  other arithmetic  8.19 us (5%)
  matrix products  5.74 us (3%)
    all_to_all x1, starting transfers between devices, body(): lax.all_to_all(slot_place, 'dp', split_axis=0, concat_axis=0, tiled=True)  29.3 us
    all_to_all x1, waiting for transfers between devices, body(): lax.all_to_all(packed, 'dp', split_axis=0, concat_axis=0, tiled=True)  23.7 us
    all_to_all x1, waiting for transfers between devices, body(): lax.all_to_all(slot_place, 'dp', split_axis=0, concat_axis=0, tiled=True)  19.4 us
    all_to_all x1, blocking collectives, body(): lax.all_to_all(widen(merged_keys), 'ctx', split_axis=1, concat_axis=0, ti...  15 us
    all_to_all x1, starting transfers between devices, body(): lax.all_to_all(query_split, 'ctx', split_axis=1, concat_axis=0, tiled=True)  12.4 us
    all_to_all x1, waiting for transfers between devices, body(): lax.all_to_all(joined, 'ctx', split_axis=0, concat_axis=1, tiled=True)  11.4 us
    all_to_all x1, waiting for transfers between devices, body(): lax.all_to_all(query_split, 'ctx', split_axis=1, concat_axis=0, tiled=True)  11 us
    all_to_all x1, waiting for transfers between devices, body(): lax.all_to_all(widen(merged_values), 'ctx', split_axis=1, concat_axis=0,...  11 us
  transfers between devices with their start and end apart: 6, of which 6 were waited for; matrix products, arithmetic and copies ran while one was open for 4% of the time, Pallas kernels for 0%

commit v1 on v0

v1 whole, which is shorter than its diff:
```python
import jax
import jax.numpy as jnp
from jax import lax
from jax.experimental import pallas as pl
from jax.experimental.pallas import tpu as pltpu
from jax.sharding import Mesh
from jax.sharding import PartitionSpec as P

HD = 128
CAP = 4
CHUNK = 512
LOG2E = 1.4426950408889634
NEVER = 512


def attend_kernel(first_ref, queries_ref, keys_values_ref, head_ref, out_ref, value_ref, top, mixed):
    rows, width = queries_ref.shape
    heads = width // HD
    factor = HD ** (-0.5) * LOG2E
    first = first_ref[0]
    top[...] = jnp.full(top.shape, -1e30, jnp.float32)
    mixed[...] = jnp.zeros(mixed.shape, jnp.float32)
    ones = jnp.ones((CHUNK, HD), jnp.bfloat16)

    def add_chunk(start, masked):
        keys = keys_values_ref[pl.ds(start, CHUNK), :HD]
        values = jnp.concatenate([keys_values_ref[pl.ds(start, CHUNK), HD:], ones], axis=1)
        if masked:
            allowed = start + lax.broadcasted_iota(jnp.int32, (rows, CHUNK), 1) <= (
                first + lax.broadcasted_iota(jnp.int32, (rows, CHUNK), 0)
            )
        for h in range(heads):
            scores = lax.dot_general(
                queries_ref[:, h * HD : (h + 1) * HD],
                keys,
                (((1,), (1,)), ((), ())),
                preferred_element_type=jnp.float32,
            )
            if masked:
                scores = jnp.where(allowed, scores, -1e30)
            before = top[:, h * HD : (h + 1) * HD]
            now = jnp.maximum(before, jnp.max(scores, axis=1, keepdims=True))
            weights = jnp.exp2((scores - now[:, :1]) * factor)
            shrink = jnp.exp2((before - now) * factor)
            top[:, h * HD : (h + 1) * HD] = now
            mixed[h] = mixed[h] * jnp.concatenate([shrink, shrink], axis=1) + jnp.dot(
                weights.astype(jnp.bfloat16), values, preferred_element_type=jnp.float32
            )

    whole = first // CHUNK

    def step(i, carry):
        add_chunk(pl.multiple_of(i * CHUNK, CHUNK), False)
        return carry

    lax.fori_loop(0, whole, step, 0)
    add_chunk(pl.multiple_of(whole * CHUNK, CHUNK), True)
    value = jnp.zeros((rows, HD), jnp.float32)
    for h in range(heads):
        total = mixed[h]
        out = (total[:, :HD] / total[:, HD:]).astype(jnp.bfloat16)
        out_ref[:, h * HD : (h + 1) * HD] = out
        value = value + out.astype(jnp.float32) * head_ref[:, h * HD : (h + 1) * HD]
    value_ref[...] = lax.dot_general(
        jnp.ones((8, HD), jnp.float32),
        value,
        (((1,), (1,)), ((), ())),
        preferred_element_type=jnp.float32,
        precision=lax.Precision.HIGHEST,
    )


def attend(first, queries, keys_values, head):
    rows, width = queries.shape
    length = keys_values.shape[0]
    vmem = pl.BlockSpec(memory_space=pltpu.VMEM)
    return pl.pallas_call(
        attend_kernel,
        out_shape=(
            jax.ShapeDtypeStruct((rows, width), jnp.bfloat16),
            jax.ShapeDtypeStruct((8, rows), jnp.float32),
        ),
        in_specs=[pl.BlockSpec(memory_space=pltpu.SMEM), vmem, vmem, vmem],
        out_specs=(vmem, vmem),
        scratch_shapes=[
            pltpu.VMEM((rows, width), jnp.float32),
            pltpu.VMEM((width // HD, rows, 2 * HD), jnp.float32),
        ],
        compiler_params=pltpu.CompilerParams(vmem_limit_bytes=32 * 2**20),
        cost_estimate=pl.CostEstimate(
            flops=4 * rows * width * length, bytes_accessed=4 * rows * width, transcendentals=rows * width * length // HD
        ),
    )(first, queries, keys_values, head)


def body(queries, keys_text, values_text, patch_rows, patch_owner, patch_place, value_head):
    rows = queries.shape[1]
    half = queries.shape[2] // 2
    dp_count = lax.axis_size("dp")
    chip_count = lax.axis_size("xh") * lax.axis_size("y")
    core = lax.axis_index("co")
    chip = lax.axis_index("xh") * lax.axis_size("y") + lax.axis_index("y")
    swap = [(0, 1), (1, 0)]

    owner = patch_owner[0, 0, :, 0]
    place = patch_place[0, 0]
    count = owner.shape[0]
    earlier = jnp.arange(count)[:, None] < jnp.arange(count)[None, :]
    rank = jnp.sum(jnp.where(earlier & (owner[:, None] == owner[None, :]), 1, 0), axis=0)
    slots = dp_count * CAP
    select = jnp.arange(slots, dtype=jnp.int32)[:, None] == (owner * CAP + rank)[None, :]
    slot_place = jnp.sum(jnp.where(select, place[None, :] - NEVER, 0), axis=1) + NEVER
    packed = jnp.dot(
        select.astype(jnp.bfloat16),
        patch_rows[0, 0].reshape(count, 4 * HD),
        preferred_element_type=jnp.float32,
    ).astype(jnp.bfloat16)
    packed = packed.reshape(dp_count, CAP, 2, 2, HD).transpose(0, 3, 1, 2, 4)
    places = jnp.broadcast_to(
        slot_place.reshape(dp_count, 1, CAP, 1, 1).astype(jnp.bfloat16), (dp_count, 2, CAP, 1, HD)
    )
    packed = jnp.concatenate([packed, places], axis=3).reshape(dp_count * 2, CAP, 3 * HD)
    arrived = lax.all_to_all(packed, ("dp", "co"), 0, 0, tiled=True)
    arrived = arrived.reshape(dp_count * 2 * CAP, 3 * HD)

    text = jnp.concatenate([keys_text[0], values_text[0]], axis=1)
    text = text.reshape(rows, 2, 2, HD)
    other_text = lax.dynamic_index_in_dim(text, 1 - core, 2, False).reshape(rows, 2 * HD)
    own_text = lax.dynamic_index_in_dim(text, core, 2, False).reshape(rows, 2 * HD)
    both_queries = queries[0]
    other_queries = lax.dynamic_slice_in_dim(both_queries, (1 - core) * half, half, 1)
    own_queries = lax.dynamic_slice_in_dim(both_queries, core * half, half, 1)
    got_text = lax.ppermute(other_text, "co", swap)
    got_queries = lax.ppermute(other_queries, "co", swap)
    head = lax.dynamic_slice_in_dim(value_head, core * half, half, 0)[None].astype(jnp.float32)
    both_text = jnp.where(
        core == 0,
        jnp.concatenate([own_text, got_text], axis=0),
        jnp.concatenate([got_text, own_text], axis=0),
    )

    sender = (jnp.arange(dp_count * 2 * CAP, dtype=jnp.int32) // CAP) % 2
    token = arrived[:, 2 * HD].astype(jnp.int32) + sender * rows
    token = jnp.where(arrived[:, 2 * HD] < rows, token, NEVER)
    landing = (jnp.arange(2 * rows, dtype=jnp.int32)[:, None] == token[None, :]).astype(jnp.bfloat16)
    merged = (
        both_text.astype(jnp.float32)
        + jnp.dot(landing, arrived[:, : 2 * HD], preferred_element_type=jnp.float32)
    ).astype(jnp.bfloat16)
    keys_values = lax.all_to_all(
        jnp.broadcast_to(merged[None], (chip_count, *merged.shape)), ("xh", "y"), 0, 0, tiled=True
    ).reshape(chip_count * 2 * rows, 2 * HD)

    start = chip * (2 * rows)
    other_out, other_value = attend((start + (1 - core) * rows)[None], got_queries, keys_values, head)
    own_out, own_value = attend((start + core * rows)[None], own_queries, keys_values, head)
    got_out = lax.ppermute(other_out, "co", swap)
    got_value = lax.ppermute(other_value[0], "co", swap)
    attention = jnp.where(
        core == 0,
        jnp.concatenate([own_out, got_out], axis=1),
        jnp.concatenate([got_out, own_out], axis=1),
    )
    partial_value = own_value[0] + got_value
    value_out = partial_value + lax.ppermute(partial_value, "tp", swap)
    return attention[None], value_out[None]


def solution(mesh):
    dp, ctx, tp = mesh.devices.shape
    wide = Mesh(mesh.devices.reshape(dp, 2, ctx // 4, 2, tp), ("dp", "xh", "y", "co", "tp"))
    ctx = ("xh", "y", "co")
    in_specs = (
        P("dp", ctx, "tp"),
        P("dp", ctx, "tp"),
        P("dp", ctx, "tp"),
        P("dp", ctx, None, None, "tp"),
        P("dp", ctx, None, None),
        P("dp", ctx, None),
        P("tp"),
    )
    out_specs = (P("dp", ctx, "tp"), P("dp", ctx))
    return jax.shard_map(body, mesh=wide, in_specs=in_specs, out_specs=out_specs, check_vma=False)
```

time: 177 us -> 121 us (0.68)
  the two profiles are of different devices: /device:TPU:1 before, /device:TPU:30 now
where the time goes in v1:
time: 121 us
  starting transfers between devices  47.7 us (39%)
  waiting for transfers between devices  46.6 us (39%)
  Pallas kernels  16.1 us (13%)
  local copies, waits for them, and re-layouts  6.41 us (5%)
  other arithmetic  2.48 us (2%)
    all_to_all x1, waiting for transfers between devices, body(): arrived = lax.all_to_all(packed, ('dp', 'co'), 0, 0, tiled=True)  34.3 us
    all_to_all x1, starting transfers between devices, body(): arrived = lax.all_to_all(packed, ('dp', 'co'), 0, 0, tiled=True)  29.5 us
    pallas_call x2, Pallas kernels, attend(): pl.pallas_call(attend_kernel, out_shape=(jax.ShapeDtypeStruct((rows, widt...  16.1 us
    all_to_all x1, waiting for transfers between devices, body(): lax.all_to_all(jnp.broadcast_to(merged[None], (chip_count, *merged.shape)...  8.74 us
    all_to_all x1, starting transfers between devices, body(): lax.all_to_all(jnp.broadcast_to(merged[None], (chip_count, *merged.shape)...  7.23 us
    unnamed x15, local copies, waits for them, and re-layouts  3.49 us
    ppermute x1, starting transfers between devices, body(): value_out = partial_value + lax.ppermute(partial_value, 'tp', swap)  2.75 us
    ppermute x1, waiting for transfers between devices, body(): value_out = partial_value + lax.ppermute(partial_value, 'tp', swap)  2.69 us
  transfers between devices with their start and end apart: 7, of which 4 were waited for; matrix products, arithmetic and copies ran while one was open for 1% of the time, Pallas kernels for 7%

profile of v1, /device:TPU:30, one launch (start us, length us, event | category | flops | bytes accessed | tf_op | source)
XLA Modules:
  0.0 120.6 jit_solution(16768954458273350738)
XLA Ops:
  0.6 0.6 copy-done.4
  1.4 0.8 copy.32
  2.2 0.3 convolution_convert_fusion
  2.7 0.5 copy-done.5
  4.2 0.8 copy.29
  5.1 29.5 %all-to-all-start = ((bf16[64,4,384]{2,1,0:T(4,128)(2,1)}), bf16[64,4,384]{2,1,0:T(4,128)(2,1)S(1)}, u32[]{:S(2)}, u32[]{:S(2)}) async-start(bf16[64,4,384]{2,1,0:T(4,128)(2,1)} %copy.29), calls=%async_computation | async-start | bytes 393216 | tf_op jit(solution)/shard_map/all_to_all | solution.py:123
  34.7 0.7 copy-done.2
  35.6 0.3 fusion.6
  35.9 2.0 %collective-permute-start = (bf16[128,256]{1,0:T(8,128)(2,1)S(1)}, bf16[128,256]{1,0:T(8,128)(2,1)S(1)}, u32[]{:S(2)}, u32[]{:S(2)}) collective-permute-start(bf16[128,256]{1,0:T(8,128)(2,1)S(1)} %bitcast.52), channel_id=1, source_target_pairs={{0,2},{2,0},{1,3},{3,1},{4,6},{6,4},{5,7},{7,5},{8,10},{10,8},{9,1... | collective-permute-start | bytes 196616 | tf_op jit(solution)/shard_map/ppermute | solution.py:133
  37.9 34.3 %all-to-all-done = bf16[64,4,384]{2,1,0:T(4,128)(2,1)S(1)} async-done(((bf16[64,4,384]{2,1,0:T(4,128)(2,1)}), bf16[64,4,384]{2,1,0:T(4,128)(2,1)S(1)}, u32[]{:S(2)}, u32[]{:S(2)}) %all-to-all-start) | async-done | bytes 196640 | tf_op jit(solution)/shard_map/all_to_all | solution.py:123
  72.8 1.0 broadcast_in_dim.59
  73.8 7.2 %all-to-all-start.1 = ((bf16[8,256,256]{2,1,0:T(8,128)(2,1)}), bf16[8,256,256]{2,1,0:T(8,128)(2,1)S(1)}, u32[]{:S(2)}, u32[]{:S(2)}) async-start(bf16[8,256,256]{2,1,0:T(8,128)(2,1)} %broadcast_in_dim.59), calls=%async_computation.1 | async-start | bytes 2097152 | tf_op jit(solution)/shard_map/all_to_all | solution.py:150
  81.1 1.9 %collective-permute-start.1 = (bf16[128,1024]{1,0:T(8,128)(2,1)S(1)}, bf16[128,1024]{1,0:T(8,128)(2,1)S(1)}, u32[]{:S(2)}, u32[]{:S(2)}) collective-permute-start(bf16[128,1024]{1,0:T(8,128)(2,1)S(1)} %get-tuple-element.11), channel_id=1, source_target_pairs={{0,2},{2,0},{1,3},{3,1},{4,6},{6,4},{5,7},{7,5},{8,10},{10,8},{9,1... | collective-permute-start | bytes 786440 | tf_op jit(solution)/shard_map/ppermute | solution.py:134
  83.0 0.7 copy-done.3
  83.7 0.8 collective-permute-done.1.queries_ref
  84.5 8.7 %all-to-all-done.1 = bf16[8,256,256]{2,1,0:T(8,128)(2,1)S(1)} async-done(((bf16[8,256,256]{2,1,0:T(8,128)(2,1)}), bf16[8,256,256]{2,1,0:T(8,128)(2,1)S(1)}, u32[]{:S(2)}, u32[]{:S(2)}) %all-to-all-start.1) | async-done | bytes 1048608 | tf_op jit(solution)/shard_map/all_to_all | solution.py:150
  93.2 8.0 %shard_map.87 = (bf16[128,1024]{1,0:T(8,128)(2,1)S(1)}, f32[8,128]{1,0:T(8,128)S(1)}) custom-call(s32[1]{0:T(128)} %bitcast.8.first_ref, bf16[128,1024]{1,0:T(8,128)(2,1)S(1)} %collective-permute-done.1.queries_ref, bf16[2048,256]{1,0:T(8,128)(2,1)S(1)} %bitcast.41, f32[1,1024]{1,0:T(1,128)S(1)} %bitcast.44), custom_call_target="tpu_custom_call" | custom-call | flops 1073741824 | bytes 524288 | tf_op jit(solution)/shard_map/pallas_call | solution.py:77
  101.3 1.9 %collective-permute-start.3 = (f32[128]{0:T(128)S(1)}, f32[128]{0:T(128)S(1)}, u32[]{:S(2)}, u32[]{:S(2)}) collective-permute-start(f32[128]{0:T(128)S(1)} %slice_bitcast_fusion), channel_id=1, source_target_pairs={{0,2},{2,0},{1,3},{3,1},{4,6},{6,4},{5,7},{7,5},{8,10},{10,8},{9,1... | collective-permute-start | bytes 1544 | tf_op jit(solution)/shard_map/ppermute | solution.py:158
  103.2 2.4 %collective-permute-start.2 = (bf16[128,1024]{1,0:T(8,128)(2,1)S(1)}, bf16[128,1024]{1,0:T(8,128)(2,1)S(1)}, u32[]{:S(2)}, u32[]{:S(2)}) collective-permute-start(bf16[128,1024]{1,0:T(8,128)(2,1)S(1)} %get-tuple-element.7), channel_id=1, source_target_pairs={{0,2},{2,0},{1,3},{3,1},{4,6},{6,4},{5,7},{7,5},{8,10},{10,8},{9,1... | collective-permute-start | bytes 786440 | tf_op jit(solution)/shard_map/ppermute | solution.py:157
  105.6 8.1 %shard_map.86 = (bf16[128,1024]{1,0:T(8,128)(2,1)S(1)}, f32[8,128]{1,0:T(8,128)S(1)}) custom-call(s32[1]{0:T(128)} %bitcast.first_ref, bf16[128,1024]{1,0:T(8,128)(2,1)S(1)} %get-tuple-element.10.queries_ref, bf16[2048,256]{1,0:T(8,128)(2,1)S(1)} %bitcast.42, f32[1,1024]{1,0:T(1,128)S(1)} %bitcast.45), custom_call_target="tpu_custom_call" | custom-call | flops 1073741824 | bytes 524288 | tf_op jit(solution)/shard_map/pallas_call | solution.py:77
  113.7 2.8 %collective-permute-start.4 = (f32[128]{0:T(128)S(1)}, f32[128]{0:T(128)S(1)}, u32[]{:S(2)}, u32[]{:S(2)}) collective-permute-start(f32[128]{0:T(128)S(1)} %bitcast_add_fusion), channel_id=1, source_target_pairs={{0,1},{1,0},{2,3},{3,2},{4,5},{5,4},{6,7},{7,6},{8,9},{9,8},{10,11... | collective-permute-start | bytes 1544 | tf_op jit(solution)/shard_map/ppermute | solution.py:165
  116.5 2.7 %collective-permute-done.4 = f32[128]{0:T(128)S(1)} collective-permute-done((f32[128]{0:T(128)S(1)}, f32[128]{0:T(128)S(1)}, u32[]{:S(2)}, u32[]{:S(2)}) %collective-permute-start.4) | collective-permute-done | bytes 544 | tf_op jit(solution)/shard_map/ppermute | solution.py:165
  119.2 0.5 add_bitcast_fusion
  119.7 0.9 maximum_select_fusion
  (38 shorter events, 2.0 us)
Async XLA Ops:
  0.6 0.7 copy-start.4
  2.6 0.7 copy-start.5
  5.1 29.5 %copy-start.1 = (bf16[1,128,256]{2,1,0:T(8,128)(2,1)S(1)}, bf16[1,128,256]{2,1,0:T(8,128)(2,1)}, u32[]{:S(2)}) copy-start(bf16[1,128,256]{2,1,0:T(8,128)(2,1)} %param.8) | copy-start | bytes 196612
  5.1 67.2 %all-to-all-start = ((bf16[64,4,384]{2,1,0:T(4,128)(2,1)}), bf16[64,4,384]{2,1,0:T(4,128)(2,1)S(1)}, u32[]{:S(2)}, u32[]{:S(2)}) async-start(bf16[64,4,384]{2,1,0:T(4,128)(2,1)} %copy.29), calls=%async_computation | async-start | bytes 393216 | tf_op jit(solution)/shard_map/all_to_all | solution.py:123
  34.6 0.8 copy-start.2
  35.9 36.6 %collective-permute-start = (bf16[128,256]{1,0:T(8,128)(2,1)S(1)}, bf16[128,256]{1,0:T(8,128)(2,1)S(1)}, u32[]{:S(2)}, u32[]{:S(2)}) collective-permute-start(bf16[128,256]{1,0:T(8,128)(2,1)S(1)} %bitcast.52), channel_id=1, source_target_pairs={{0,2},{2,0},{1,3},{3,1},{4,6},{6,4},{5,7},{7,5},{8,10},{10,8},{9,1... | collective-permute-start | bytes 196616 | tf_op jit(solution)/shard_map/ppermute | solution.py:133
  73.8 7.2 %copy-start = (bf16[1,128,2048]{2,1,0:T(8,128)(2,1)S(1)}, bf16[1,128,2048]{2,1,0:T(8,128)(2,1)}, u32[]{:S(2)}) copy-start(bf16[1,128,2048]{2,1,0:T(8,128)(2,1)} %param.7) | copy-start | bytes 1572868
  73.8 19.4 %all-to-all-start.1 = ((bf16[8,256,256]{2,1,0:T(8,128)(2,1)}), bf16[8,256,256]{2,1,0:T(8,128)(2,1)S(1)}, u32[]{:S(2)}, u32[]{:S(2)}) async-start(bf16[8,256,256]{2,1,0:T(8,128)(2,1)} %broadcast_in_dim.59), calls=%async_computation.1 | async-start | bytes 2097152 | tf_op jit(solution)/shard_map/all_to_all | solution.py:150
  81.1 3.4 %collective-permute-start.1 = (bf16[128,1024]{1,0:T(8,128)(2,1)S(1)}, bf16[128,1024]{1,0:T(8,128)(2,1)S(1)}, u32[]{:S(2)}, u32[]{:S(2)}) collective-permute-start(bf16[128,1024]{1,0:T(8,128)(2,1)S(1)} %get-tuple-element.11), channel_id=1, source_target_pairs={{0,2},{2,0},{1,3},{3,1},{4,6},{6,4},{5,7},{7,5},{8,10},{10,8},{9,1... | collective-permute-start | bytes 786440 | tf_op jit(solution)/shard_map/ppermute | solution.py:134
  83.0 0.7 copy-start.3
  101.3 12.4 %collective-permute-start.3 = (f32[128]{0:T(128)S(1)}, f32[128]{0:T(128)S(1)}, u32[]{:S(2)}, u32[]{:S(2)}) collective-permute-start(f32[128]{0:T(128)S(1)} %slice_bitcast_fusion), channel_id=1, source_target_pairs={{0,2},{2,0},{1,3},{3,1},{4,6},{6,4},{5,7},{7,5},{8,10},{10,8},{9,1... | collective-permute-start | bytes 1544 | tf_op jit(solution)/shard_map/ppermute | solution.py:158
  103.2 16.4 %collective-permute-start.2 = (bf16[128,1024]{1,0:T(8,128)(2,1)S(1)}, bf16[128,1024]{1,0:T(8,128)(2,1)S(1)}, u32[]{:S(2)}, u32[]{:S(2)}) collective-permute-start(bf16[128,1024]{1,0:T(8,128)(2,1)S(1)} %get-tuple-element.7), channel_id=1, source_target_pairs={{0,2},{2,0},{1,3},{3,1},{4,6},{6,4},{5,7},{7,5},{8,10},{10,8},{9,1... | collective-permute-start | bytes 786440 | tf_op jit(solution)/shard_map/ppermute | solution.py:157
  113.7 5.5 %collective-permute-start.4 = (f32[128]{0:T(128)S(1)}, f32[128]{0:T(128)S(1)}, u32[]{:S(2)}, u32[]{:S(2)}) collective-permute-start(f32[128]{0:T(128)S(1)} %bitcast_add_fusion), channel_id=1, source_target_pairs={{0,1},{1,0},{2,3},{3,2},{4,5},{5,4},{6,7},{7,6},{8,9},{9,8},{10,11... | collective-permute-start | bytes 1544 | tf_op jit(solution)/shard_map/ppermute | solution.py:165

commit v2 on v1

v2 whole, which is shorter than its diff:
```python
import jax
import jax.numpy as jnp
from jax import lax
from jax.experimental import pallas as pl
from jax.experimental.pallas import tpu as pltpu
from jax.sharding import Mesh
from jax.sharding import PartitionSpec as P

HD = 128
CAP = 4
CHUNK = 512
LOG2E = 1.4426950408889634


def column(row):
    count = row.shape[1]
    same = lax.broadcasted_iota(jnp.int32, (count, count), 0) == lax.broadcasted_iota(
        jnp.int32, (count, count), 1
    )
    return jnp.sum(jnp.where(same, row, 0), axis=1, keepdims=True)


def pack_kernel(patch_ref, owner_ref, place_ref, out_ref):
    owner, place = owner_ref[...], place_ref[...]
    count = owner.shape[1]
    owner_column = column(owner)
    earlier = lax.broadcasted_iota(jnp.int32, (count, count), 1) < lax.broadcasted_iota(
        jnp.int32, (count, count), 0
    )
    rank = jnp.sum(jnp.where(earlier & (owner_column == owner), 1, 0), axis=1, keepdims=True)
    target = owner_column * CAP + rank
    patch, row = (
        lax.broadcasted_iota(jnp.int32, (count, 2 * count), 0),
        lax.broadcasted_iota(jnp.int32, (count, 2 * count), 1),
    )
    target = jnp.sum(jnp.where(patch == row // 2, target, 0), axis=0, keepdims=True)
    row, patch = (
        lax.broadcasted_iota(jnp.int32, (2 * count, count), 0),
        lax.broadcasted_iota(jnp.int32, (2 * count, count), 1),
    )
    code = jnp.sum(jnp.where(patch == row // 2, place + 1, 0), axis=1, keepdims=True)
    rows = out_ref.shape[0]
    out, row = (
        lax.broadcasted_iota(jnp.int32, (rows, 2 * count), 0),
        lax.broadcasted_iota(jnp.int32, (rows, 2 * count), 1),
    )
    select = (out // 2 == target) & (out % 2 == row % 2)
    held = jnp.concatenate(
        [
            patch_ref[...],
            jnp.broadcast_to(code.astype(jnp.float32), (2 * count, HD)).astype(jnp.bfloat16),
        ],
        axis=1,
    )
    select = jnp.where(select, 1.0, 0.0).astype(jnp.bfloat16)
    out_ref[...] = jnp.dot(select, held, preferred_element_type=jnp.float32).astype(jnp.bfloat16)


def pack(patch_rows, owner, place, sequences):
    vmem = pl.BlockSpec(memory_space=pltpu.VMEM)
    return pl.pallas_call(
        pack_kernel,
        out_shape=jax.ShapeDtypeStruct((sequences * CAP * 2, patch_rows.shape[1] + HD), jnp.bfloat16),
        in_specs=[vmem, vmem, vmem],
        out_specs=vmem,
    )(patch_rows, owner, place)


def attend_kernel(first_ref, queries_ref, keys_values_ref, head_ref, out_ref, *value_ref):
    rows, width = queries_ref.shape
    length = keys_values_ref.shape[0]
    factor = HD ** (-0.5) * LOG2E
    first = first_ref[0]

    def attend_first(count):
        keys = keys_values_ref[:count, :HD]
        values = jnp.concatenate(
            [keys_values_ref[:count, HD:], jnp.ones((count, HD), jnp.bfloat16)], axis=1
        )
        whole = count - CHUNK
        allowed = whole + lax.broadcasted_iota(jnp.int32, (rows, CHUNK), 1) <= (
            first + lax.broadcasted_iota(jnp.int32, (rows, CHUNK), 0)
        )
        value = jnp.zeros((rows, HD), jnp.float32)
        for lower in range(0, width, HD):
            scores = lax.dot_general(
                queries_ref[:, lower : lower + HD],
                keys,
                (((1,), (1,)), ((), ())),
                preferred_element_type=jnp.float32,
            )
            last = jnp.where(allowed, scores[:, whole:], -1e30)
            scores = jnp.concatenate([scores[:, :whole], last], axis=1) if whole else last
            top = jnp.max(scores, axis=1, keepdims=True)
            weights = jnp.exp2((scores - top) * factor).astype(jnp.bfloat16)
            mixed = jnp.dot(weights, values, preferred_element_type=jnp.float32)
            out = (mixed[:, :HD] / mixed[:, HD:]).astype(jnp.bfloat16)
            out_ref[:rows, lower : lower + HD] = out
            value = value + out.astype(jnp.float32) * head_ref[:, lower : lower + HD]
        total = lax.dot_general(
            jnp.ones((16, HD), jnp.float32),
            value,
            (((1,), (1,)), ((), ())),
            preferred_element_type=jnp.float32,
            precision=lax.Precision.HIGHEST,
        )
        if value_ref:
            value_ref[0][...] = total
        else:
            row = lax.broadcasted_iota(jnp.int32, total.shape, 0)
            high = total.astype(jnp.bfloat16).astype(jnp.float32)
            middle = (total - high).astype(jnp.bfloat16).astype(jnp.float32)
            pieces = jnp.where(row == 0, high, jnp.where(row == 1, middle, total - high - middle))
            out_ref[rows:, :HD] = pieces.astype(jnp.bfloat16)
            out_ref[rows:, HD:] = jnp.zeros((16, width - HD), jnp.bfloat16)

    for i in range(length // CHUNK):

        @pl.when(first // CHUNK == i)
        def _():
            attend_first((i + 1) * CHUNK)


def attend(first, queries, keys_values, head, sums_apart):
    rows, width = queries.shape
    length = keys_values.shape[0]
    vmem = pl.BlockSpec(memory_space=pltpu.VMEM)
    out_shape = [jax.ShapeDtypeStruct((rows if sums_apart else rows + 16, width), jnp.bfloat16)]
    if sums_apart:
        out_shape.append(jax.ShapeDtypeStruct((16, rows), jnp.float32))
    return pl.pallas_call(
        attend_kernel,
        out_shape=out_shape,
        in_specs=[pl.BlockSpec(memory_space=pltpu.SMEM), vmem, vmem, vmem],
        out_specs=[vmem] * len(out_shape),
        compiler_params=pltpu.CompilerParams(vmem_limit_bytes=32 * 2**20),
        cost_estimate=pl.CostEstimate(
            flops=4 * rows * width * length, bytes_accessed=4 * rows * width, transcendentals=rows * width * length // HD
        ),
    )(first, queries, keys_values, head)


def body(queries, keys_text, values_text, patch_rows, patch_owner, patch_place, value_head):
    rows = queries.shape[1]
    half = queries.shape[2] // 2
    dp_count = lax.axis_size("dp")
    chip_count = lax.axis_size("xh") * lax.axis_size("y")
    core = lax.axis_index("co")
    chip = lax.axis_index("xh") * lax.axis_size("y") + lax.axis_index("y")
    swap = [(0, 1), (1, 0)]
    count = patch_rows.shape[2]

    packed = pack(
        patch_rows.reshape(count * 2, 2 * HD),
        patch_owner.reshape(1, count),
        patch_place.reshape(1, count),
        dp_count,
    )
    arrived = lax.all_to_all(packed.reshape(dp_count, CAP * 2, 3 * HD), "dp", 0, 0, tiled=True)
    arrived = arrived.reshape(dp_count * CAP * 2, 3 * HD)
    code = arrived[:, 2 * HD].astype(jnp.int32)
    is_value = jnp.arange(code.shape[0], dtype=jnp.int32) % 2
    lands = (jnp.arange(rows, dtype=jnp.int32)[:, None] + 1) == code[None, :]

    def merge(text, wanted):
        landing = jnp.where(lands & (is_value == wanted)[None, :], 1.0, 0.0).astype(jnp.bfloat16)
        added = jnp.dot(landing, arrived[:, : 2 * HD], preferred_element_type=jnp.float32)
        return (text[0].astype(jnp.float32) + added).astype(jnp.bfloat16)

    merged_keys, merged_values = merge(keys_text, 0), merge(values_text, 1)

    def of_head(which):
        return jnp.concatenate(
            [
                jnp.where(which == 0, tensor[:, :HD], tensor[:, HD:])
                for tensor in (merged_keys, merged_values)
            ],
            axis=1,
        )

    own_merged = of_head(core)
    got_merged = lax.ppermute(of_head(1 - core), "co", swap)
    merged = jnp.where(
        core == 0,
        jnp.concatenate([own_merged, got_merged], axis=0),
        jnp.concatenate([got_merged, own_merged], axis=0),
    )
    other_queries = lax.dynamic_slice_in_dim(queries[0], (1 - core) * half, half, 1)
    own_queries = lax.dynamic_slice_in_dim(queries[0], core * half, half, 1)
    got_queries = lax.ppermute(other_queries, "co", swap)
    head = lax.dynamic_slice_in_dim(value_head, core * half, half, 0)[None].astype(jnp.float32)

    keys_values = lax.all_to_all(
        jnp.broadcast_to(merged[None], (chip_count, *merged.shape)), ("xh", "y"), 0, 0, tiled=True
    ).reshape(chip_count * 2 * rows, 2 * HD)

    start = chip * (2 * rows)
    (other_out,) = attend((start + (1 - core) * rows)[None], got_queries, keys_values, head, False)
    own_out, own_value = attend((start + core * rows)[None], own_queries, keys_values, head, True)
    got_out = lax.ppermute(other_out, "co", swap)
    got_value = jnp.sum(got_out[rows : rows + 3, :HD].astype(jnp.float32), axis=0)
    attention = jnp.where(
        core == 0,
        jnp.concatenate([own_out, got_out[:rows]], axis=1),
        jnp.concatenate([got_out[:rows], own_out], axis=1),
    )
    partial_value = own_value[0] + got_value
    far_value = lax.ppermute(partial_value, "tp", swap)
    attention, far_value = lax.optimization_barrier((attention, far_value))
    return attention[None], (partial_value + far_value)[None]


def solution(mesh):
    dp, ctx, tp = mesh.devices.shape
    wide = Mesh(mesh.devices.reshape(dp, 2, ctx // 4, 2, tp), ("dp", "xh", "y", "co", "tp"))
    ctx = ("xh", "y", "co")
    in_specs = (
        P("dp", ctx, "tp"),
        P("dp", ctx, "tp"),
        P("dp", ctx, "tp"),
        P("dp", ctx, None, None, "tp"),
        P("dp", ctx, None, None),
        P("dp", ctx, None),
        P("tp"),
    )
    out_specs = (P("dp", ctx, "tp"), P("dp", ctx))
    return jax.shard_map(body, mesh=wide, in_specs=in_specs, out_specs=out_specs, check_vma=False)
```

time: 121 us -> 111 us (0.917)
  the two profiles are of different devices: /device:TPU:30 before, /device:TPU:1 now
where the time goes in v2:
time: 111 us; the launch traced here: 109 us
  starting transfers between devices  49 us (44%)
  waiting for transfers between devices  48.6 us (44%)
  Pallas kernels  4.59 us (4%)
  local copies, waits for them, and re-layouts  3.89 us (4%)
  other arithmetic  1.65 us (1%)
    all_to_all x1, waiting for transfers between devices, body(): lax.all_to_all(packed.reshape(dp_count, CAP * 2, 3 * HD), 'dp', 0, 0, til...  35.4 us
    all_to_all x1, starting transfers between devices, body(): lax.all_to_all(packed.reshape(dp_count, CAP * 2, 3 * HD), 'dp', 0, 0, til...  29.3 us
    all_to_all x1, waiting for transfers between devices, body(): lax.all_to_all(jnp.broadcast_to(merged[None], (chip_count, *merged.shape)...  10.8 us
    all_to_all x1, starting transfers between devices, body(): lax.all_to_all(jnp.broadcast_to(merged[None], (chip_count, *merged.shape)...  6.78 us
    ppermute x1, starting transfers between devices, body(): got_merged = lax.ppermute(of_head(1 - core), 'co', swap)  4.3 us
    ppermute x1, starting transfers between devices, body(): got_out = lax.ppermute(other_out, 'co', swap)  3.88 us
    pallas_call x2, Pallas kernels, attend(): pl.pallas_call(attend_kernel, out_shape=out_shape, in_specs=[pl.BlockSpec...  2.68 us
    ppermute x1, starting transfers between devices, body(): got_queries = lax.ppermute(other_queries, 'co', swap)  2.54 us
  transfers between devices with their start and end apart: 6, of which 5 were waited for; matrix products, arithmetic and copies ran while one was open for 1% of the time, Pallas kernels for 1%

profile of v2, /device:TPU:1, one launch (start us, length us, event | category | flops | bytes accessed | tf_op | source)
XLA Modules:
  0.0 109.0 jit_solution(511834909510719715)
XLA Ops:
  0.6 1.5 %reshape.84.patch_ref = bf16[128,256]{1,0:T(8,128)(2,1)} reshape(bf16[1,1,64,2,256]{4,3,2,1,0:T(2,128)(2,1)} %param.10) | data formatting | bytes 131072 | tf_op jit(solution)/shard_map/reshape | solution.py:154
  2.1 1.9 %shard_map.86 = bf16[256,384]{1,0:T(8,128)(2,1)} custom-call(bf16[128,256]{1,0:T(8,128)(2,1)} %reshape.84.patch_ref, s32[1,64]{1,0:T(1,128)} %bitcast.32, s32[1,64]{1,0:T(1,128)} %bitcast.33), custom_call_target="tpu_custom_call" | custom-call | tf_op jit(solution)/shard_map/pallas_call | solution.py:61
  4.0 29.3 %all-to-all-start = ((bf16[32,8,384]{2,1,0:T(8,128)(2,1)}), bf16[32,8,384]{2,1,0:T(8,128)(2,1)S(1)}, u32[]{:S(2)}, u32[]{:S(2)}) async-start(bf16[32,8,384]{2,1,0:T(8,128)(2,1)} %bitcast.27), calls=%async_computation | async-start | bytes 393216 | tf_op jit(solution)/shard_map/all_to_all | solution.py:159
  33.3 0.0 copy-start.2
  33.4 35.4 %all-to-all-done = bf16[32,8,384]{2,1,0:T(8,128)(2,1)S(1)} async-done(((bf16[32,8,384]{2,1,0:T(8,128)(2,1)}), bf16[32,8,384]{2,1,0:T(8,128)(2,1)S(1)}, u32[]{:S(2)}, u32[]{:S(2)}) %all-to-all-start) | async-done | bytes 196640 | tf_op jit(solution)/shard_map/all_to_all | solution.py:159
  68.8 0.1 convert_reduce_fusion
  68.9 0.2 fusion
  69.1 0.6 copy-done.3
  69.8 0.2 fusion.1
  70.0 4.3 %collective-permute-start = (bf16[128,256]{1,0:T(8,128)(2,1)S(1)}, bf16[128,256]{1,0:T(8,128)(2,1)S(1)}, u32[]{:S(2)}, u32[]{:S(2)}) collective-permute-start(bf16[128,256]{1,0:T(8,128)(2,1)S(1)} %pad_maximum_fusion), channel_id=1, source_target_pairs={{0,2},{2,0},{1,3},{3,1},{4,6},{6,4},{5,7},{7,5},{8,10},{10,8},{9,1... | collective-permute-start | bytes 196616 | tf_op jit(solution)/shard_map/ppermute | solution.py:182
  74.3 0.9 collective-permute-done
  75.2 1.0 broadcast_in_dim.36
  76.3 6.8 %all-to-all-start.1 = ((bf16[8,256,256]{2,1,0:T(8,128)(2,1)}), bf16[8,256,256]{2,1,0:T(8,128)(2,1)S(1)}, u32[]{:S(2)}, u32[]{:S(2)}) async-start(bf16[8,256,256]{2,1,0:T(8,128)(2,1)} %broadcast_in_dim.36), calls=%async_computation.1 | async-start | bytes 2097152 | tf_op jit(solution)/shard_map/all_to_all | solution.py:193
  83.1 2.5 %collective-permute-start.1 = (bf16[128,1024]{1,0:T(8,128)(2,1)S(1)}, bf16[128,1024]{1,0:T(8,128)(2,1)S(1)}, u32[]{:S(2)}, u32[]{:S(2)}) collective-permute-start(bf16[128,1024]{1,0:T(8,128)(2,1)S(1)} %get-tuple-element.11), channel_id=1, source_target_pairs={{0,2},{2,0},{1,3},{3,1},{4,6},{6,4},{5,7},{7,5},{8,10},{10,8},{9,1... | collective-permute-start | bytes 786440 | tf_op jit(solution)/shard_map/ppermute | solution.py:190
  85.7 0.7 copy-done.1
  86.4 0.4 collective-permute-done.1.queries_ref
  86.8 10.8 %all-to-all-done.1 = bf16[8,256,256]{2,1,0:T(8,128)(2,1)S(1)} async-done(((bf16[8,256,256]{2,1,0:T(8,128)(2,1)}), bf16[8,256,256]{2,1,0:T(8,128)(2,1)S(1)}, u32[]{:S(2)}, u32[]{:S(2)}) %all-to-all-start.1) | async-done | bytes 1048608 | tf_op jit(solution)/shard_map/all_to_all | solution.py:193
  97.6 1.3 %shard_map.88 = bf16[144,1024]{1,0:T(8,128)(2,1)S(1)} custom-call(s32[1]{0:T(128)} %bitcast.10.first_ref, bf16[128,1024]{1,0:T(8,128)(2,1)S(1)} %collective-permute-done.1.queries_ref, bf16[2048,256]{1,0:T(8,128)(2,1)S(1)} %bitcast.23, f32[1,1024]{1,0:T(1,128)S(1)} %bitcast.25), custom_call_target="tpu_custom_call" | custom-call | flops 1073741824 | bytes 524288 | tf_op jit(solution)/shard_map/pallas_call | solution.py:131
  98.9 3.9 %collective-permute-start.2 = (bf16[144,1024]{1,0:T(8,128)(2,1)S(1)}, bf16[144,1024]{1,0:T(8,128)(2,1)S(1)}, u32[]{:S(2)}, u32[]{:S(2)}) collective-permute-start(bf16[144,1024]{1,0:T(8,128)(2,1)S(1)} %shard_map.88), channel_id=1, source_target_pairs={{0,2},{2,0},{1,3},{3,1},{4,6},{6,4},{5,7},{7,5},{8,10},{10,8},{9,1... | collective-permute-start | bytes 884744 | tf_op jit(solution)/shard_map/ppermute | solution.py:200
  102.8 1.4 %shard_map.87 = (bf16[128,1024]{1,0:T(8,128)(2,1)S(1)}, f32[16,128]{1,0:T(8,128)S(1)}) custom-call(s32[1]{0:T(128)} %bitcast.first_ref, bf16[128,1024]{1,0:T(8,128)(2,1)S(1)} %get-tuple-element.10.queries_ref, bf16[2048,256]{1,0:T(8,128)(2,1)S(1)} %bitcast.24, f32[1,1024]{1,0:T(1,128)S(1)} %bitcast.26), custom_call_target="tpu_custom_call" | custom-call | flops 1073741824 | bytes 524288 | tf_op jit(solution)/shard_map/pallas_call | solution.py:131
  104.2 2.2 %collective-permute-start.3 = (f32[128]{0:T(128)S(1)}, f32[128]{0:T(128)S(1)}, u32[]{:S(2)}, u32[]{:S(2)}) collective-permute-start(f32[128]{0:T(128)S(1)} %bitcast_add_fusion), channel_id=1, source_target_pairs={{0,1},{1,0},{2,3},{3,2},{4,5},{5,4},{6,7},{7,6},{8,9},{9,8},{10,11... | collective-permute-start | bytes 1544 | tf_op jit(solution)/shard_map/ppermute | solution.py:208
  106.5 0.9 maximum_select_fusion
  107.4 1.1 %collective-permute-done.3 = f32[128]{0:T(128)S(1)} collective-permute-done((f32[128]{0:T(128)S(1)}, f32[128]{0:T(128)S(1)}, u32[]{:S(2)}, u32[]{:S(2)}) %collective-permute-start.3) | collective-permute-done | bytes 544 | tf_op jit(solution)/shard_map/ppermute | solution.py:208
  108.5 0.5 add_bitcast_fusion
  (17 shorter events, 0.2 us)
Async XLA Ops:
  4.0 64.7 %all-to-all-start = ((bf16[32,8,384]{2,1,0:T(8,128)(2,1)}), bf16[32,8,384]{2,1,0:T(8,128)(2,1)S(1)}, u32[]{:S(2)}, u32[]{:S(2)}) async-start(bf16[32,8,384]{2,1,0:T(8,128)(2,1)} %bitcast.27), calls=%async_computation | async-start | bytes 393216 | tf_op jit(solution)/shard_map/all_to_all | solution.py:159
  33.3 35.6 %copy-start.2 = (bf16[1,128,256]{2,1,0:T(8,128)(2,1)S(1)}, bf16[1,128,256]{2,1,0:T(8,128)(2,1)}, u32[]{:S(2)}) copy-start(bf16[1,128,256]{2,1,0:T(8,128)(2,1)} %param.8) | copy-start | bytes 196612
  68.9 0.8 copy-start.3
  70.0 5.2 %collective-permute-start = (bf16[128,256]{1,0:T(8,128)(2,1)S(1)}, bf16[128,256]{1,0:T(8,128)(2,1)S(1)}, u32[]{:S(2)}, u32[]{:S(2)}) collective-permute-start(bf16[128,256]{1,0:T(8,128)(2,1)S(1)} %pad_maximum_fusion), channel_id=1, source_target_pairs={{0,2},{2,0},{1,3},{3,1},{4,6},{6,4},{5,7},{7,5},{8,10},{10,8},{9,1... | collective-permute-start | bytes 196616 | tf_op jit(solution)/shard_map/ppermute | solution.py:182
  76.3 6.8 %copy-start = (bf16[1,128,2048]{2,1,0:T(8,128)(2,1)S(1)}, bf16[1,128,2048]{2,1,0:T(8,128)(2,1)}, u32[]{:S(2)}) copy-start(bf16[1,128,2048]{2,1,0:T(8,128)(2,1)} %param.7) | copy-start | bytes 1572868
  76.3 21.3 %all-to-all-start.1 = ((bf16[8,256,256]{2,1,0:T(8,128)(2,1)}), bf16[8,256,256]{2,1,0:T(8,128)(2,1)S(1)}, u32[]{:S(2)}, u32[]{:S(2)}) async-start(bf16[8,256,256]{2,1,0:T(8,128)(2,1)} %broadcast_in_dim.36), calls=%async_computation.1 | async-start | bytes 2097152 | tf_op jit(solution)/shard_map/all_to_all | solution.py:193
  83.1 3.7 %collective-permute-start.1 = (bf16[128,1024]{1,0:T(8,128)(2,1)S(1)}, bf16[128,1024]{1,0:T(8,128)(2,1)S(1)}, u32[]{:S(2)}, u32[]{:S(2)}) collective-permute-start(bf16[128,1024]{1,0:T(8,128)(2,1)S(1)} %get-tuple-element.11), channel_id=1, source_target_pairs={{0,2},{2,0},{1,3},{3,1},{4,6},{6,4},{5,7},{7,5},{8,10},{10,8},{9,1... | collective-permute-start | bytes 786440 | tf_op jit(solution)/shard_map/ppermute | solution.py:190
  85.7 0.7 copy-start.1
  98.9 5.3 %collective-permute-start.2 = (bf16[144,1024]{1,0:T(8,128)(2,1)S(1)}, bf16[144,1024]{1,0:T(8,128)(2,1)S(1)}, u32[]{:S(2)}, u32[]{:S(2)}) collective-permute-start(bf16[144,1024]{1,0:T(8,128)(2,1)S(1)} %shard_map.88), channel_id=1, source_target_pairs={{0,2},{2,0},{1,3},{3,1},{4,6},{6,4},{5,7},{7,5},{8,10},{10,8},{9,1... | collective-permute-start | bytes 884744 | tf_op jit(solution)/shard_map/ppermute | solution.py:200
  104.2 4.3 %collective-permute-start.3 = (f32[128]{0:T(128)S(1)}, f32[128]{0:T(128)S(1)}, u32[]{:S(2)}, u32[]{:S(2)}) collective-permute-start(f32[128]{0:T(128)S(1)} %bitcast_add_fusion), channel_id=1, source_target_pairs={{0,1},{1,0},{2,3},{3,2},{4,5},{5,4},{6,7},{7,6},{8,9},{9,8},{10,11... | collective-permute-start | bytes 1544 | tf_op jit(solution)/shard_map/ppermute | solution.py:208

commit v3 on v2

--- a/solution.py
+++ b/solution.py
@@ -24,43 +24,26 @@
     owner, place = owner_ref[...], place_ref[...]
     count = owner.shape[1]
     owner_column = column(owner)
-    earlier = lax.broadcasted_iota(jnp.int32, (count, count), 1) < lax.broadcasted_iota(
-        jnp.int32, (count, count), 0
-    )
-    rank = jnp.sum(jnp.where(earlier & (owner_column == owner), 1, 0), axis=1, keepdims=True)
-    target = owner_column * CAP + rank
-    patch, row = (
-        lax.broadcasted_iota(jnp.int32, (count, 2 * count), 0),
-        lax.broadcasted_iota(jnp.int32, (count, 2 * count), 1),
-    )
-    target = jnp.sum(jnp.where(patch == row // 2, target, 0), axis=0, keepdims=True)
-    row, patch = (
-        lax.broadcasted_iota(jnp.int32, (2 * count, count), 0),
-        lax.broadcasted_iota(jnp.int32, (2 * count, count), 1),
-    )
-    code = jnp.sum(jnp.where(patch == row // 2, place + 1, 0), axis=1, keepdims=True)
-    rows = out_ref.shape[0]
-    out, row = (
-        lax.broadcasted_iota(jnp.int32, (rows, 2 * count), 0),
-        lax.broadcasted_iota(jnp.int32, (rows, 2 * count), 1),
-    )
-    select = (out // 2 == target) & (out % 2 == row % 2)
-    held = jnp.concatenate(
-        [
-            patch_ref[...],
-            jnp.broadcast_to(code.astype(jnp.float32), (2 * count, HD)).astype(jnp.bfloat16),
-        ],
-        axis=1,
-    )
-    select = jnp.where(select, 1.0, 0.0).astype(jnp.bfloat16)
-    out_ref[...] = jnp.dot(select, held, preferred_element_type=jnp.float32).astype(jnp.bfloat16)
+    earlier = lax.broadcasted_iota(jnp.int32, (count, count), 0) < lax.broadcasted_iota(
+        jnp.int32, (count, count), 1
+    )
+    rank = jnp.sum(jnp.where(earlier & (owner_column == owner), 1, 0), axis=0, keepdims=True)
+    target = owner * CAP + rank
+    code = jnp.broadcast_to((column(place) + 1).astype(jnp.float32), (count, HD)).astype(jnp.bfloat16)
+    row = lax.broadcasted_iota(jnp.int32, (out_ref.shape[0], count), 0)
+    packed = jnp.zeros(out_ref.shape, jnp.float32)
+    for which in range(2):
+        select = jnp.where((row // 2 == target) & (row % 2 == which), 1.0, 0.0).astype(jnp.bfloat16)
+        held = jnp.concatenate([patch_ref[:, which, :], code], axis=1)
+        packed = packed + jnp.dot(select, held, preferred_element_type=jnp.float32)
+    out_ref[...] = packed.astype(jnp.bfloat16)
 
 
 def pack(patch_rows, owner, place, sequences):
     vmem = pl.BlockSpec(memory_space=pltpu.VMEM)
     return pl.pallas_call(
         pack_kernel,
-        out_shape=jax.ShapeDtypeStruct((sequences * CAP * 2, patch_rows.shape[1] + HD), jnp.bfloat16),
+        out_shape=jax.ShapeDtypeStruct((sequences * CAP * 2, patch_rows.shape[2] + HD), jnp.bfloat16),
         in_specs=[vmem, vmem, vmem],
         out_specs=vmem,
     )(patch_rows, owner, place)
@@ -151,23 +134,32 @@
     count = patch_rows.shape[2]
 
     packed = pack(
-        patch_rows.reshape(count * 2, 2 * HD),
+        patch_rows[0, 0],
         patch_owner.reshape(1, count),
         patch_place.reshape(1, count),
         dp_count,
     )
     arrived = lax.all_to_all(packed.reshape(dp_count, CAP * 2, 3 * HD), "dp", 0, 0, tiled=True)
     arrived = arrived.reshape(dp_count * CAP * 2, 3 * HD)
+    other_queries = lax.dynamic_slice_in_dim(queries[0], (1 - core) * half, half, 1)
+    own_queries = lax.dynamic_slice_in_dim(queries[0], core * half, half, 1)
+    got_queries = lax.ppermute(other_queries, "co", swap)
+    head = lax.dynamic_slice_in_dim(value_head, core * half, half, 0)[None].astype(jnp.float32)
+    text = jnp.concatenate([keys_text[0], values_text[0]], axis=1)
+    arrived, got_queries, own_queries, head, text = lax.optimization_barrier(
+        (arrived, got_queries, own_queries, head, text)
+    )
+
     code = arrived[:, 2 * HD].astype(jnp.int32)
     is_value = jnp.arange(code.shape[0], dtype=jnp.int32) % 2
     lands = (jnp.arange(rows, dtype=jnp.int32)[:, None] + 1) == code[None, :]
 
-    def merge(text, wanted):
+    def added(wanted):
         landing = jnp.where(lands & (is_value == wanted)[None, :], 1.0, 0.0).astype(jnp.bfloat16)
-        added = jnp.dot(landing, arrived[:, : 2 * HD], preferred_element_type=jnp.float32)
-        return (text[0].astype(jnp.float32) + added).astype(jnp.bfloat16)
-
-    merged_keys, merged_values = merge(keys_text, 0), merge(values_text, 1)
+        return jnp.dot(landing, arrived[:, : 2 * HD], preferred_element_type=jnp.float32)
+
+    merged_keys = (text[:, : 2 * HD].astype(jnp.float32) + added(0)).astype(jnp.bfloat16)
+    merged_values = (text[:, 2 * HD :].astype(jnp.float32) + added(1)).astype(jnp.bfloat16)
 
     def of_head(which):
         return jnp.concatenate(
@@ -185,11 +177,6 @@
         jnp.concatenate([own_merged, got_merged], axis=0),
         jnp.concatenate([got_merged, own_merged], axis=0),
     )
-    other_queries = lax.dynamic_slice_in_dim(queries[0], (1 - core) * half, half, 1)
-    own_queries = lax.dynamic_slice_in_dim(queries[0], core * half, half, 1)
-    got_queries = lax.ppermute(other_queries, "co", swap)
-    head = lax.dynamic_slice_in_dim(value_head, core * half, half, 0)[None].astype(jnp.float32)
-
     keys_values = lax.all_to_all(
         jnp.broadcast_to(merged[None], (chip_count, *merged.shape)), ("xh", "y"), 0, 0, tiled=True
     ).reshape(chip_count * 2 * rows, 2 * HD)

time: 111 us -> 109 us (0.982)
  local copies, waits for them, and re-layouts: 3.89 us -> 1.76 us
    all_to_all x1, waiting for transfers between devices: 35.4 us -> 31.4 us  [body(): lax.all_to_all(packed.reshape(dp_count, CAP * 2, 3 * HD), 'dp', 0, 0, til...]
    all_to_all x1, waiting for transfers between devices: 10.8 us -> 14.5 us  [body(): lax.all_to_all(jnp.broadcast_to(merged[None], (chip_count, *merged.shape)...]
    reshape x1 -> x0, local copies, waits for them, and re-layouts: 1.49 us -> none  [body(): patch_rows.reshape(count * 2, 2 * HD)]
where the time goes in v3:
time: 109 us; the launch traced here: 107 us
  starting transfers between devices  49.2 us (45%)
  waiting for transfers between devices  48.3 us (44%)
  Pallas kernels  4.75 us (4%)
  local copies, waits for them, and re-layouts  1.76 us (2%)
  other arithmetic  1.66 us (2%)
    all_to_all x1, waiting for transfers between devices, body(): lax.all_to_all(packed.reshape(dp_count, CAP * 2, 3 * HD), 'dp', 0, 0, til...  31.4 us
    all_to_all x1, starting transfers between devices, body(): lax.all_to_all(packed.reshape(dp_count, CAP * 2, 3 * HD), 'dp', 0, 0, til...  29.3 us
    all_to_all x1, waiting for transfers between devices, body(): lax.all_to_all(jnp.broadcast_to(merged[None], (chip_count, *merged.shape)...  14.5 us
    all_to_all x1, starting transfers between devices, body(): lax.all_to_all(jnp.broadcast_to(merged[None], (chip_count, *merged.shape)...  6.65 us
    ppermute x1, starting transfers between devices, body(): got_merged = lax.ppermute(of_head(1 - core), 'co', swap)  4.3 us
    ppermute x1, starting transfers between devices, body(): got_out = lax.ppermute(other_out, 'co', swap)  3.87 us
    ppermute x1, starting transfers between devices, body(): got_queries = lax.ppermute(other_queries, 'co', swap)  2.86 us
    pallas_call x2, Pallas kernels, attend(): pl.pallas_call(attend_kernel, out_shape=out_shape, in_specs=[pl.BlockSpec...  2.77 us
  transfers between devices with their start and end apart: 6, of which 5 were waited for; matrix products, arithmetic and copies ran while one was open for 1% of the time, Pallas kernels for 1%

profile of v3, /device:TPU:1, one launch (start us, length us, event | category | flops | bytes accessed | tf_op | source)
XLA Modules:
  0.0 106.9 jit_solution(8484642645573603532)
XLA Ops:
  0.6 2.0 %shard_map.86 = bf16[256,384]{1,0:T(8,128)(2,1)} custom-call(bf16[64,2,256]{2,1,0:T(2,128)(2,1)} %bitcast.29, s32[1,64]{1,0:T(1,128)} %bitcast.32, s32[1,64]{1,0:T(1,128)} %bitcast.33), custom_call_target="tpu_custom_call" | custom-call | tf_op jit(solution)/shard_map/pallas_call | solution.py:44
  2.6 29.3 %all-to-all-start = ((bf16[32,8,384]{2,1,0:T(8,128)(2,1)}), bf16[32,8,384]{2,1,0:T(8,128)(2,1)S(1)}, u32[]{:S(2)}, u32[]{:S(2)}) async-start(bf16[32,8,384]{2,1,0:T(8,128)(2,1)} %bitcast.24), calls=%async_computation | async-start | bytes 393216 | tf_op jit(solution)/shard_map/all_to_all | solution.py:142
  31.9 0.0 copy-start.1
  31.9 0.0 copy-start.2
  32.0 2.9 %collective-permute-start = (bf16[128,1024]{1,0:T(8,128)(2,1)S(1)}, bf16[128,1024]{1,0:T(8,128)(2,1)S(1)}, u32[]{:S(2)}, u32[]{:S(2)}) collective-permute-start(bf16[128,1024]{1,0:T(8,128)(2,1)S(1)} %get-tuple-element.21), channel_id=1, source_target_pairs={{0,2},{2,0},{1,3},{3,1},{4,6},{6,4},{5,7},{7,5},{8,10},{10,8},{9,1... | collective-permute-start | bytes 786440 | tf_op jit(solution)/shard_map/ppermute | solution.py:146
  34.9 0.0 copy-start.3
  34.9 0.6 copy-done.3
  35.6 0.4 collective-permute-done.queries_ref
  36.0 31.4 %all-to-all-done = bf16[32,8,384]{2,1,0:T(8,128)(2,1)S(1)} async-done(((bf16[32,8,384]{2,1,0:T(8,128)(2,1)}), bf16[32,8,384]{2,1,0:T(8,128)(2,1)S(1)}, u32[]{:S(2)}, u32[]{:S(2)}) %all-to-all-start) | async-done | bytes 196640 | tf_op jit(solution)/shard_map/all_to_all | solution.py:142
  67.4 0.1 convert_reduce_fusion
  67.5 0.2 add_convert_fusion
  67.7 0.2 add_convert_fusion.1
  68.0 4.3 %collective-permute-start.1 = (bf16[128,256]{1,0:T(8,128)(2,1)S(1)}, bf16[128,256]{1,0:T(8,128)(2,1)S(1)}, u32[]{:S(2)}, u32[]{:S(2)}) collective-permute-start(bf16[128,256]{1,0:T(8,128)(2,1)S(1)} %pad_maximum_fusion.1), channel_id=1, source_target_pairs={{0,2},{2,0},{1,3},{3,1},{4,6},{6,4},{5,7},{7,5},{8,10},{10,8},{9,1... | collective-permute-start | bytes 196616 | tf_op jit(solution)/shard_map/ppermute | solution.py:174
  72.3 0.9 collective-permute-done.1
  73.2 1.0 broadcast_in_dim.36
  74.2 6.7 %all-to-all-start.1 = ((bf16[8,256,256]{2,1,0:T(8,128)(2,1)}), bf16[8,256,256]{2,1,0:T(8,128)(2,1)S(1)}, u32[]{:S(2)}, u32[]{:S(2)}) async-start(bf16[8,256,256]{2,1,0:T(8,128)(2,1)} %broadcast_in_dim.36), calls=%async_computation.1 | async-start | bytes 2097152 | tf_op jit(solution)/shard_map/all_to_all | solution.py:180
  80.9 14.5 %all-to-all-done.1 = bf16[8,256,256]{2,1,0:T(8,128)(2,1)S(1)} async-done(((bf16[8,256,256]{2,1,0:T(8,128)(2,1)}), bf16[8,256,256]{2,1,0:T(8,128)(2,1)S(1)}, u32[]{:S(2)}, u32[]{:S(2)}) %all-to-all-start.1) | async-done | bytes 1048608 | tf_op jit(solution)/shard_map/all_to_all | solution.py:180
  95.4 1.3 %shard_map.88 = bf16[144,1024]{1,0:T(8,128)(2,1)S(1)} custom-call(s32[1]{0:T(128)} %bitcast.12.first_ref, bf16[128,1024]{1,0:T(8,128)(2,1)S(1)} %collective-permute-done.queries_ref, bf16[2048,256]{1,0:T(8,128)(2,1)S(1)} %bitcast.20, f32[1,1024]{1,0:T(1,128)S(1)} %bitcast.22), custom_call_target="tpu_custom_call" | custom-call | flops 1073741824 | bytes 524288 | tf_op jit(solution)/shard_map/pallas_call | solution.py:114
  96.8 3.9 %collective-permute-start.2 = (bf16[144,1024]{1,0:T(8,128)(2,1)S(1)}, bf16[144,1024]{1,0:T(8,128)(2,1)S(1)}, u32[]{:S(2)}, u32[]{:S(2)}) collective-permute-start(bf16[144,1024]{1,0:T(8,128)(2,1)S(1)} %shard_map.88), channel_id=1, source_target_pairs={{0,2},{2,0},{1,3},{3,1},{4,6},{6,4},{5,7},{7,5},{8,10},{10,8},{9,1... | collective-permute-start | bytes 884744 | tf_op jit(solution)/shard_map/ppermute | solution.py:187
  100.6 1.4 %shard_map.87 = (bf16[128,1024]{1,0:T(8,128)(2,1)S(1)}, f32[16,128]{1,0:T(8,128)S(1)}) custom-call(s32[1]{0:T(128)} %bitcast.first_ref, bf16[128,1024]{1,0:T(8,128)(2,1)S(1)} %get-tuple-element.11.queries_ref, bf16[2048,256]{1,0:T(8,128)(2,1)S(1)} %bitcast.21, f32[1,1024]{1,0:T(1,128)S(1)} %bitcast.23), custom_call_target="tpu_custom_call" | custom-call | flops 1073741824 | bytes 524288 | tf_op jit(solution)/shard_map/pallas_call | solution.py:114
  102.1 2.3 %collective-permute-start.3 = (f32[128]{0:T(128)S(1)}, f32[128]{0:T(128)S(1)}, u32[]{:S(2)}, u32[]{:S(2)}) collective-permute-start(f32[128]{0:T(128)S(1)} %bitcast_add_fusion), channel_id=1, source_target_pairs={{0,1},{1,0},{2,3},{3,2},{4,5},{5,4},{6,7},{7,6},{8,9},{9,8},{10,11... | collective-permute-start | bytes 1544 | tf_op jit(solution)/shard_map/ppermute | solution.py:195
  104.4 0.9 maximum_select_fusion
  105.3 1.1 %collective-permute-done.3 = f32[128]{0:T(128)S(1)} collective-permute-done((f32[128]{0:T(128)S(1)}, f32[128]{0:T(128)S(1)}, u32[]{:S(2)}, u32[]{:S(2)}) %collective-permute-start.3) | collective-permute-done | bytes 544 | tf_op jit(solution)/shard_map/ppermute | solution.py:195
  106.4 0.5 add_bitcast_fusion
  (17 shorter events, 0.2 us)
Async XLA Ops:
  0.6 31.3 %copy-start = (bf16[1,128,2048]{2,1,0:T(8,128)(2,1)S(1)}, bf16[1,128,2048]{2,1,0:T(8,128)(2,1)}, u32[]{:S(2)}) copy-start(bf16[1,128,2048]{2,1,0:T(8,128)(2,1)} %param.7) | copy-start | bytes 1572868
  2.6 64.7 %all-to-all-start = ((bf16[32,8,384]{2,1,0:T(8,128)(2,1)}), bf16[32,8,384]{2,1,0:T(8,128)(2,1)S(1)}, u32[]{:S(2)}, u32[]{:S(2)}) async-start(bf16[32,8,384]{2,1,0:T(8,128)(2,1)} %bitcast.24), calls=%async_computation | async-start | bytes 393216 | tf_op jit(solution)/shard_map/all_to_all | solution.py:142
  31.9 3.7 %copy-start.1 = (bf16[1,128,256]{2,1,0:T(8,128)(2,1)S(1)}, bf16[1,128,256]{2,1,0:T(8,128)(2,1)}, u32[]{:S(2)}) copy-start(bf16[1,128,256]{2,1,0:T(8,128)(2,1)} %param.9) | copy-start | bytes 196612
  31.9 3.6 %copy-start.2 = (bf16[1,128,256]{2,1,0:T(8,128)(2,1)S(1)}, bf16[1,128,256]{2,1,0:T(8,128)(2,1)}, u32[]{:S(2)}) copy-start(bf16[1,128,256]{2,1,0:T(8,128)(2,1)} %param.8) | copy-start | bytes 196612
  32.0 4.0 %collective-permute-start = (bf16[128,1024]{1,0:T(8,128)(2,1)S(1)}, bf16[128,1024]{1,0:T(8,128)(2,1)S(1)}, u32[]{:S(2)}, u32[]{:S(2)}) collective-permute-start(bf16[128,1024]{1,0:T(8,128)(2,1)S(1)} %get-tuple-element.21), channel_id=1, source_target_pairs={{0,2},{2,0},{1,3},{3,1},{4,6},{6,4},{5,7},{7,5},{8,10},{10,8},{9,1... | collective-permute-start | bytes 786440 | tf_op jit(solution)/shard_map/ppermute | solution.py:146
  34.9 0.7 copy-start.3
  68.0 5.2 %collective-permute-start.1 = (bf16[128,256]{1,0:T(8,128)(2,1)S(1)}, bf16[128,256]{1,0:T(8,128)(2,1)S(1)}, u32[]{:S(2)}, u32[]{:S(2)}) collective-permute-start(bf16[128,256]{1,0:T(8,128)(2,1)S(1)} %pad_maximum_fusion.1), channel_id=1, source_target_pairs={{0,2},{2,0},{1,3},{3,1},{4,6},{6,4},{5,7},{7,5},{8,10},{10,8},{9,1... | collective-permute-start | bytes 196616 | tf_op jit(solution)/shard_map/ppermute | solution.py:174
  74.2 21.2 %all-to-all-start.1 = ((bf16[8,256,256]{2,1,0:T(8,128)(2,1)}), bf16[8,256,256]{2,1,0:T(8,128)(2,1)S(1)}, u32[]{:S(2)}, u32[]{:S(2)}) async-start(bf16[8,256,256]{2,1,0:T(8,128)(2,1)} %broadcast_in_dim.36), calls=%async_computation.1 | async-start | bytes 2097152 | tf_op jit(solution)/shard_map/all_to_all | solution.py:180
  96.8 5.3 %collective-permute-start.2 = (bf16[144,1024]{1,0:T(8,128)(2,1)S(1)}, bf16[144,1024]{1,0:T(8,128)(2,1)S(1)}, u32[]{:S(2)}, u32[]{:S(2)}) collective-permute-start(bf16[144,1024]{1,0:T(8,128)(2,1)S(1)} %shard_map.88), channel_id=1, source_target_pairs={{0,2},{2,0},{1,3},{3,1},{4,6},{6,4},{5,7},{7,5},{8,10},{10,8},{9,1... | collective-permute-start | bytes 884744 | tf_op jit(solution)/shard_map/ppermute | solution.py:187
  102.1 4.3 %collective-permute-start.3 = (f32[128]{0:T(128)S(1)}, f32[128]{0:T(128)S(1)}, u32[]{:S(2)}, u32[]{:S(2)}) collective-permute-start(f32[128]{0:T(128)S(1)} %bitcast_add_fusion), channel_id=1, source_target_pairs={{0,1},{1,0},{2,3},{3,2},{4,5},{5,4},{6,7},{7,6},{8,9},{9,8},{10,11... | collective-permute-start | bytes 1544 | tf_op jit(solution)/shard_map/ppermute | solution.py:195

commit v4 on v3

--- a/solution.py
+++ b/solution.py
@@ -177,13 +177,17 @@
         jnp.concatenate([own_merged, got_merged], axis=0),
         jnp.concatenate([got_merged, own_merged], axis=0),
     )
-    keys_values = lax.all_to_all(
-        jnp.broadcast_to(merged[None], (chip_count, *merged.shape)), ("xh", "y"), 0, 0, tiled=True
-    ).reshape(chip_count * 2 * rows, 2 * HD)
-
+    wide = jnp.broadcast_to(merged[None], (chip_count, *merged.shape))
     start = chip * (2 * rows)
-    (other_out,) = attend((start + (1 - core) * rows)[None], got_queries, keys_values, head, False)
-    own_out, own_value = attend((start + core * rows)[None], own_queries, keys_values, head, True)
+    firsts = (start + (1 - core) * rows)[None], (start + core * rows)[None]
+    wide, got_queries, own_queries, head, firsts = lax.optimization_barrier(
+        (wide, got_queries, own_queries, head, firsts)
+    )
+    keys_values = lax.all_to_all(wide, ("xh", "y"), 0, 0, tiled=True)
+    keys_values = keys_values.reshape(chip_count * 2 * rows, 2 * HD)
+
+    (other_out,) = attend(firsts[0], got_queries, keys_values, head, False)
+    own_out, own_value = attend(firsts[1], own_queries, keys_values, head, True)
     got_out = lax.ppermute(other_out, "co", swap)
     got_value = jnp.sum(got_out[rows : rows + 3, :HD].astype(jnp.float32), axis=0)
     attention = jnp.where(

time: 109 us -> 108 us (level); the launches traced: 107 us -> 107 us
  blocking collectives: 0 us -> 22.1 us
  waiting for transfers between devices: 48.3 us -> 33.7 us
  starting transfers between devices: 49.2 us -> 43 us
    all_to_all x0 -> x1, blocking collectives: none -> 22.1 us  [body(): keys_values = lax.all_to_all(wide, ('xh', 'y'), 0, 0, tiled=True)]
    all_to_all x1 -> x0, waiting for transfers between devices: 14.5 us -> none  [body(): lax.all_to_all(jnp.broadcast_to(merged[None], (chip_count, *merged.shape)...]
    all_to_all x1 -> x0, starting transfers between devices: 6.65 us -> none  [body(): lax.all_to_all(jnp.broadcast_to(merged[None], (chip_count, *merged.shape)...]
  transfers between devices with their start and end apart: 6 -> 5, of which waited for: 5 -> 4; matrix products, arithmetic and copies ran while one was open for 1% -> 1% of each run, Pallas kernels for 1% -> 1%
where the time goes in v4:
time: 108 us; the launch traced here: 107 us
  starting transfers between devices  43 us (40%)
  waiting for transfers between devices  33.7 us (31%)
  blocking collectives  22.1 us (20%)
  Pallas kernels  4.65 us (4%)
  other arithmetic  1.66 us (2%)
    all_to_all x1, waiting for transfers between devices, body(): lax.all_to_all(packed.reshape(dp_count, CAP * 2, 3 * HD), 'dp', 0, 0, til...  31.4 us
    all_to_all x1, starting transfers between devices, body(): lax.all_to_all(packed.reshape(dp_count, CAP * 2, 3 * HD), 'dp', 0, 0, til...  29.3 us
    all_to_all x1, blocking collectives, body(): keys_values = lax.all_to_all(wide, ('xh', 'y'), 0, 0, tiled=True)  22.1 us
    ppermute x1, starting transfers between devices, body(): got_out = lax.ppermute(other_out, 'co', swap)  4.37 us
    ppermute x1, starting transfers between devices, body(): got_merged = lax.ppermute(of_head(1 - core), 'co', swap)  4.3 us
    ppermute x1, starting transfers between devices, body(): got_queries = lax.ppermute(other_queries, 'co', swap)  2.86 us
    pallas_call x2, Pallas kernels, attend(): pl.pallas_call(attend_kernel, out_shape=out_shape, in_specs=[pl.BlockSpec...  2.68 us
    ppermute x1, starting transfers between devices, body(): far_value = lax.ppermute(partial_value, 'tp', swap)  2.22 us
  transfers between devices with their start and end apart: 5, of which 4 were waited for; matrix products, arithmetic and copies ran while one was open for 1% of the time, Pallas kernels for 1%

profile of v4, /device:TPU:1, one launch (start us, length us, event | category | flops | bytes accessed | tf_op | source)
XLA Modules:
  0.0 107.3 jit_solution(5198826108067081772)
XLA Ops:
  0.6 2.0 %shard_map.86 = bf16[256,384]{1,0:T(8,128)(2,1)} custom-call(bf16[64,2,256]{2,1,0:T(2,128)(2,1)} %bitcast.29, s32[1,64]{1,0:T(1,128)} %bitcast.32, s32[1,64]{1,0:T(1,128)} %bitcast.33), custom_call_target="tpu_custom_call" | custom-call | tf_op jit(solution)/shard_map/pallas_call | solution.py:44
  2.6 29.3 %all-to-all-start = ((bf16[32,8,384]{2,1,0:T(8,128)(2,1)}), bf16[32,8,384]{2,1,0:T(8,128)(2,1)S(1)}, u32[]{:S(2)}, u32[]{:S(2)}) async-start(bf16[32,8,384]{2,1,0:T(8,128)(2,1)} %bitcast.24), calls=%async_computation | async-start | bytes 393216 | tf_op jit(solution)/shard_map/all_to_all | solution.py:142
  31.9 0.0 copy-start.1
  31.9 0.0 copy-start.2
  32.0 2.9 %collective-permute-start = (bf16[128,1024]{1,0:T(8,128)(2,1)S(1)}, bf16[128,1024]{1,0:T(8,128)(2,1)S(1)}, u32[]{:S(2)}, u32[]{:S(2)}) collective-permute-start(bf16[128,1024]{1,0:T(8,128)(2,1)S(1)} %get-tuple-element.33), channel_id=1, source_target_pairs={{0,2},{2,0},{1,3},{3,1},{4,6},{6,4},{5,7},{7,5},{8,10},{10,8},{9,1... | collective-permute-start | bytes 786440 | tf_op jit(solution)/shard_map/ppermute | solution.py:146
  34.9 0.0 copy-start.3
  34.9 0.6 copy-done.3
  35.6 0.4 collective-permute-done.queries_ref
  36.0 31.4 %all-to-all-done = bf16[32,8,384]{2,1,0:T(8,128)(2,1)S(1)} async-done(((bf16[32,8,384]{2,1,0:T(8,128)(2,1)}), bf16[32,8,384]{2,1,0:T(8,128)(2,1)S(1)}, u32[]{:S(2)}, u32[]{:S(2)}) %all-to-all-start) | async-done | bytes 196640 | tf_op jit(solution)/shard_map/all_to_all | solution.py:142
  67.4 0.1 convert_reduce_fusion
  67.5 0.2 add_convert_fusion
  67.7 0.2 add_convert_fusion.1
  68.0 4.3 %collective-permute-start.1 = (bf16[128,256]{1,0:T(8,128)(2,1)S(1)}, bf16[128,256]{1,0:T(8,128)(2,1)S(1)}, u32[]{:S(2)}, u32[]{:S(2)}) collective-permute-start(bf16[128,256]{1,0:T(8,128)(2,1)S(1)} %pad_maximum_fusion.1), channel_id=1, source_target_pairs={{0,2},{2,0},{1,3},{3,1},{4,6},{6,4},{5,7},{7,5},{8,10},{10,8},{9,1... | collective-permute-start | bytes 196616 | tf_op jit(solution)/shard_map/ppermute | solution.py:174
  72.3 0.9 collective-permute-done.1
  73.2 0.1 broadcast_in_dim.35
  73.3 22.1 %all_to_all.10 = bf16[8,256,256]{2,1,0:T(8,128)(2,1)S(1)} all-to-all(bf16[8,256,256]{2,1,0:T(8,128)(2,1)S(1)} %broadcast_in_dim.35), channel_id=1, replica_groups=mesh['dp'=32,'xh'=2,'y'=4,'co'=2,'tp'=2] {'xh','y'}, dimensions={0} | all-to-all | bytes 2097152 | tf_op jit(solution)/shard_map/all_to_all | solution.py:186
  95.4 1.3 %shard_map.88 = bf16[144,1024]{1,0:T(8,128)(2,1)S(1)} custom-call(s32[1]{0:T(128)} %bitcast.10.first_ref, bf16[128,1024]{1,0:T(8,128)(2,1)S(1)} %collective-permute-done.queries_ref, bf16[2048,256]{1,0:T(8,128)(2,1)S(1)} %bitcast.20, f32[1,1024]{1,0:T(1,128)S(1)} %bitcast.22), custom_call_target="tpu_custom_call" | custom-call | flops 1073741824 | bytes 524288 | tf_op jit(solution)/shard_map/pallas_call | solution.py:114
  96.7 4.4 %collective-permute-start.2 = (bf16[144,1024]{1,0:T(8,128)(2,1)S(1)}, bf16[144,1024]{1,0:T(8,128)(2,1)S(1)}, u32[]{:S(2)}, u32[]{:S(2)}) collective-permute-start(bf16[144,1024]{1,0:T(8,128)(2,1)S(1)} %shard_map.88), channel_id=1, source_target_pairs={{0,2},{2,0},{1,3},{3,1},{4,6},{6,4},{5,7},{7,5},{8,10},{10,8},{9,1... | collective-permute-start | bytes 884744 | tf_op jit(solution)/shard_map/ppermute | solution.py:191
  101.0 1.4 %shard_map.87 = (bf16[128,1024]{1,0:T(8,128)(2,1)S(1)}, f32[16,128]{1,0:T(8,128)S(1)}) custom-call(s32[1]{0:T(128)} %bitcast.11.first_ref, bf16[128,1024]{1,0:T(8,128)(2,1)S(1)} %get-tuple-element.23.queries_ref, bf16[2048,256]{1,0:T(8,128)(2,1)S(1)} %bitcast.21, f32[1,1024]{1,0:T(1,128)S(1)} %bitcast.23), custom_call_target="tpu_custom_call" | custom-call | flops 1073741824 | bytes 524288 | tf_op jit(solution)/shard_map/pallas_call | solution.py:114
  102.4 0.0 collective-permute-done.2
  102.5 2.2 %collective-permute-start.3 = (f32[128]{0:T(128)S(1)}, f32[128]{0:T(128)S(1)}, u32[]{:S(2)}, u32[]{:S(2)}) collective-permute-start(f32[128]{0:T(128)S(1)} %bitcast_add_fusion), channel_id=1, source_target_pairs={{0,1},{1,0},{2,3},{3,2},{4,5},{5,4},{6,7},{7,6},{8,9},{9,8},{10,11... | collective-permute-start | bytes 1544 | tf_op jit(solution)/shard_map/ppermute | solution.py:199
  104.7 0.9 maximum_select_fusion
  105.6 1.1 %collective-permute-done.3 = f32[128]{0:T(128)S(1)} collective-permute-done((f32[128]{0:T(128)S(1)}, f32[128]{0:T(128)S(1)}, u32[]{:S(2)}, u32[]{:S(2)}) %collective-permute-start.3) | collective-permute-done | bytes 544 | tf_op jit(solution)/shard_map/ppermute | solution.py:199
  106.8 0.5 add_bitcast_fusion
  (16 shorter events, 0.2 us)
Async XLA Ops:
  0.6 31.3 %copy-start = (bf16[1,128,2048]{2,1,0:T(8,128)(2,1)S(1)}, bf16[1,128,2048]{2,1,0:T(8,128)(2,1)}, u32[]{:S(2)}) copy-start(bf16[1,128,2048]{2,1,0:T(8,128)(2,1)} %param.7) | copy-start | bytes 1572868
  2.6 64.7 %all-to-all-start = ((bf16[32,8,384]{2,1,0:T(8,128)(2,1)}), bf16[32,8,384]{2,1,0:T(8,128)(2,1)S(1)}, u32[]{:S(2)}, u32[]{:S(2)}) async-start(bf16[32,8,384]{2,1,0:T(8,128)(2,1)} %bitcast.24), calls=%async_computation | async-start | bytes 393216 | tf_op jit(solution)/shard_map/all_to_all | solution.py:142
  31.9 3.7 %copy-start.1 = (bf16[1,128,256]{2,1,0:T(8,128)(2,1)S(1)}, bf16[1,128,256]{2,1,0:T(8,128)(2,1)}, u32[]{:S(2)}) copy-start(bf16[1,128,256]{2,1,0:T(8,128)(2,1)} %param.9) | copy-start | bytes 196612
  31.9 3.6 %copy-start.2 = (bf16[1,128,256]{2,1,0:T(8,128)(2,1)S(1)}, bf16[1,128,256]{2,1,0:T(8,128)(2,1)}, u32[]{:S(2)}) copy-start(bf16[1,128,256]{2,1,0:T(8,128)(2,1)} %param.8) | copy-start | bytes 196612
  32.0 4.0 %collective-permute-start = (bf16[128,1024]{1,0:T(8,128)(2,1)S(1)}, bf16[128,1024]{1,0:T(8,128)(2,1)S(1)}, u32[]{:S(2)}, u32[]{:S(2)}) collective-permute-start(bf16[128,1024]{1,0:T(8,128)(2,1)S(1)} %get-tuple-element.33), channel_id=1, source_target_pairs={{0,2},{2,0},{1,3},{3,1},{4,6},{6,4},{5,7},{7,5},{8,10},{10,8},{9,1... | collective-permute-start | bytes 786440 | tf_op jit(solution)/shard_map/ppermute | solution.py:146
  34.9 0.7 copy-start.3
  68.0 5.2 %collective-permute-start.1 = (bf16[128,256]{1,0:T(8,128)(2,1)S(1)}, bf16[128,256]{1,0:T(8,128)(2,1)S(1)}, u32[]{:S(2)}, u32[]{:S(2)}) collective-permute-start(bf16[128,256]{1,0:T(8,128)(2,1)S(1)} %pad_maximum_fusion.1), channel_id=1, source_target_pairs={{0,2},{2,0},{1,3},{3,1},{4,6},{6,4},{5,7},{7,5},{8,10},{10,8},{9,1... | collective-permute-start | bytes 196616 | tf_op jit(solution)/shard_map/ppermute | solution.py:174
  96.7 5.8 %collective-permute-start.2 = (bf16[144,1024]{1,0:T(8,128)(2,1)S(1)}, bf16[144,1024]{1,0:T(8,128)(2,1)S(1)}, u32[]{:S(2)}, u32[]{:S(2)}) collective-permute-start(bf16[144,1024]{1,0:T(8,128)(2,1)S(1)} %shard_map.88), channel_id=1, source_target_pairs={{0,2},{2,0},{1,3},{3,1},{4,6},{6,4},{5,7},{7,5},{8,10},{10,8},{9,1... | collective-permute-start | bytes 884744 | tf_op jit(solution)/shard_map/ppermute | solution.py:191
  102.5 4.3 %collective-permute-start.3 = (f32[128]{0:T(128)S(1)}, f32[128]{0:T(128)S(1)}, u32[]{:S(2)}, u32[]{:S(2)}) collective-permute-start(f32[128]{0:T(128)S(1)} %bitcast_add_fusion), channel_id=1, source_target_pairs={{0,1},{1,0},{2,3},{3,2},{4,5},{5,4},{6,7},{7,6},{8,9},{9,8},{10,11... | collective-permute-start | bytes 1544 | tf_op jit(solution)/shard_map/ppermute | solution.py:199

commit v5 on v3

v5 whole, which is shorter than its diff:
```python
import jax
import jax.numpy as jnp
from jax import lax
from jax.experimental import pallas as pl
from jax.experimental.pallas import tpu as pltpu
from jax.sharding import Mesh
from jax.sharding import PartitionSpec as P

HD = 128
CAP = 4
CHUNK = 256
LOG2E = 1.4426950408889634


def column(row):
    count = row.shape[1]
    same = lax.broadcasted_iota(jnp.int32, (count, count), 0) == lax.broadcasted_iota(
        jnp.int32, (count, count), 1
    )
    return jnp.sum(jnp.where(same, row, 0), axis=1, keepdims=True)


def pack_kernel(patch_ref, owner_ref, place_ref, out_ref):
    owner, place = owner_ref[...], place_ref[...]
    count = owner.shape[1]
    owner_column = column(owner)
    earlier = lax.broadcasted_iota(jnp.int32, (count, count), 0) < lax.broadcasted_iota(
        jnp.int32, (count, count), 1
    )
    rank = jnp.sum(jnp.where(earlier & (owner_column == owner), 1, 0), axis=0, keepdims=True)
    code = jnp.broadcast_to((column(place) + 1).astype(jnp.float32), (count, HD)).astype(jnp.bfloat16)
    slot = lax.broadcasted_iota(jnp.int32, (out_ref.shape[0] * CAP, count), 0)
    select = jnp.where(slot == owner * CAP + rank, 1.0, 0.0).astype(jnp.bfloat16)
    held = jnp.concatenate([patch_ref[:, 0, :], patch_ref[:, 1, :], code], axis=1)
    packed = jnp.dot(select, held, preferred_element_type=jnp.float32)
    out_ref[...] = packed.reshape(out_ref.shape).astype(jnp.bfloat16)


def pack(patch_rows, owner, place, sequences):
    vmem = pl.BlockSpec(memory_space=pltpu.VMEM)
    width = patch_rows.shape[1] * patch_rows.shape[2] + HD
    return pl.pallas_call(
        pack_kernel,
        out_shape=jax.ShapeDtypeStruct((sequences, CAP, width), jnp.bfloat16),
        in_specs=[vmem, vmem, vmem],
        out_specs=vmem,
    )(patch_rows, owner, place)


def merge_kernel(arrived_ref, keys_ref, values_ref, out_ref):
    arrived = arrived_ref[...].astype(jnp.float32)
    arrived = arrived.reshape(arrived.shape[0] * arrived.shape[1], arrived.shape[2])
    width = arrived.shape[1] - HD
    token = lax.broadcasted_iota(jnp.int32, (arrived.shape[0], HD), 1).astype(jnp.float32) + 1.0
    landing = jnp.where(arrived[:, width:] == token, 1.0, 0.0).astype(jnp.bfloat16)
    added = lax.dot_general(
        landing,
        arrived[:, :width].astype(jnp.bfloat16),
        (((0,), (0,)), ((), ())),
        preferred_element_type=jnp.float32,
    )
    text = jnp.concatenate([keys_ref[...], values_ref[...]], axis=1).astype(jnp.float32)
    merged = (text + added).astype(jnp.bfloat16)
    for chip in range(out_ref.shape[0]):
        out_ref[chip] = merged


def merge(arrived, keys_text, values_text, chips):
    vmem = pl.BlockSpec(memory_space=pltpu.VMEM)
    rows, width = keys_text.shape
    return pl.pallas_call(
        merge_kernel,
        out_shape=jax.ShapeDtypeStruct((chips, rows, 2 * width), jnp.bfloat16),
        in_specs=[vmem, vmem, vmem],
        out_specs=vmem,
        compiler_params=pltpu.CompilerParams(vmem_limit_bytes=8 * 2**20),
    )(arrived, keys_text, values_text)


def attend_kernel(place_ref, queries_ref, own_ref, got_ref, head_ref, out_ref, value_ref):
    rows, width = queries_ref.shape
    length = own_ref.shape[0]
    groups = own_ref.shape[1] // (2 * HD)
    heads = width // HD
    factor = HD ** (-0.5) * LOG2E
    chip, core = place_ref[0], place_ref[1]

    def attend_first(count):
        whole = count - CHUNK
        key = lax.broadcasted_iota(jnp.int32, (rows, CHUNK), 1) + whole
        query = lax.broadcasted_iota(jnp.int32, (rows, CHUNK), 0)
        block, spot = key // rows, key % rows
        own_allowed = (block < chip) | ((block == chip) & (spot <= query))
        got_allowed = block < chip + core
        value = jnp.zeros((rows, HD), jnp.float32)
        for h in range(heads):
            g = h // (heads // groups)
            queries = queries_ref[:, h * HD : (h + 1) * HD]
            scores = []
            for ref, allowed in ((own_ref, own_allowed), (got_ref, got_allowed)):
                part = lax.dot_general(
                    queries,
                    ref[:count, g * HD : (g + 1) * HD],
                    (((1,), (1,)), ((), ())),
                    preferred_element_type=jnp.float32,
                )
                if whole:
                    scores.append(part[:, :whole])
                scores.append(jnp.where(allowed, part[:, whole:], -1e30))
            scores = jnp.concatenate(scores, axis=1)
            top = jnp.max(scores, axis=1, keepdims=True)
            weights = jnp.exp2((scores - top) * factor).astype(jnp.bfloat16)
            lower = (groups + g) * HD
            values = jnp.concatenate(
                [own_ref[:count, lower : lower + HD], got_ref[:count, lower : lower + HD]], axis=0
            )
            values = jnp.concatenate([values, jnp.ones((2 * count, HD), jnp.bfloat16)], axis=1)
            mixed = jnp.dot(weights, values, preferred_element_type=jnp.float32)
            out = (mixed[:, :HD] / mixed[:, HD:]).astype(jnp.bfloat16)
            out_ref[:, h * HD : (h + 1) * HD] = out
            value = value + out.astype(jnp.float32) * head_ref[:, h * HD : (h + 1) * HD]
        value_ref[...] = lax.dot_general(
            jnp.ones((8, HD), jnp.float32),
            value,
            (((1,), (1,)), ((), ())),
            preferred_element_type=jnp.float32,
            precision=lax.Precision.HIGHEST,
        )

    for i in range(length // CHUNK):

        @pl.when(chip // (CHUNK // rows) == i)
        def _():
            attend_first((i + 1) * CHUNK)


def attend(place, queries, own, got, head):
    rows, width = queries.shape
    vmem = pl.BlockSpec(memory_space=pltpu.VMEM)
    pairs = 2 * rows * width * own.shape[0]
    return pl.pallas_call(
        attend_kernel,
        out_shape=(
            jax.ShapeDtypeStruct((rows, width), jnp.bfloat16),
            jax.ShapeDtypeStruct((8, rows), jnp.float32),
        ),
        in_specs=[pl.BlockSpec(memory_space=pltpu.SMEM), vmem, vmem, vmem, vmem],
        out_specs=(vmem, vmem),
        compiler_params=pltpu.CompilerParams(vmem_limit_bytes=40 * 2**20),
        cost_estimate=pl.CostEstimate(
            flops=4 * pairs, bytes_accessed=4 * rows * width, transcendentals=pairs // HD
        ),
    )(place, queries, own, got, head)


def body(queries, keys_text, values_text, patch_rows, patch_owner, patch_place, value_head):
    rows = queries.shape[1]
    dp_count = lax.axis_size("dp")
    chip_count = lax.axis_size("xh") * lax.axis_size("y")
    core = lax.axis_index("co")
    chip = lax.axis_index("xh") * lax.axis_size("y") + lax.axis_index("y")
    swap = [(0, 1), (1, 0)]
    count = patch_rows.shape[2]
    width = 2 * keys_text.shape[2]

    packed = pack(
        patch_rows[0, 0],
        patch_owner.reshape(1, count),
        patch_place.reshape(1, count),
        dp_count,
    )
    arrived = lax.all_to_all(packed, "dp", 0, 0, tiled=True)
    own_queries = queries[0]
    head = value_head[None].astype(jnp.float32)
    place = jnp.stack([chip, core])
    arrived, own_queries, head, place, keys_text, values_text = lax.optimization_barrier(
        (arrived, own_queries, head, place, keys_text, values_text)
    )
    wide = merge(arrived, keys_text[0], values_text[0], chip_count)
    wide, own_queries, head, place = lax.optimization_barrier((wide, own_queries, head, place))
    own = lax.all_to_all(wide, ("xh", "y"), 0, 0, tiled=True).reshape(chip_count * rows, width)
    got = lax.ppermute(own, "co", swap)
    attention, value = attend(place, own_queries, own, got, head)
    partial_value = value[0]
    value_out = partial_value + lax.ppermute(partial_value, "tp", swap)
    return attention[None], value_out[None]


def solution(mesh):
    dp, ctx, tp = mesh.devices.shape
    wide = Mesh(mesh.devices.reshape(dp, 2, ctx // 4, 2, tp), ("dp", "xh", "y", "co", "tp"))
    ctx = ("xh", "y", "co")
    in_specs = (
        P("dp", ctx, "tp"),
        P("dp", ctx, "tp"),
        P("dp", ctx, "tp"),
        P("dp", ctx, None, None, "tp"),
        P("dp", ctx, None, None),
        P("dp", ctx, None),
        P("tp"),
    )
    out_specs = (P("dp", ctx, "tp"), P("dp", ctx))
    return jax.shard_map(body, mesh=wide, in_specs=in_specs, out_specs=out_specs, check_vma=False)
```

time: 109 us -> 103 us (0.945)
  blocking collectives: 0 us -> 20.5 us
  waiting for transfers between devices: 48.3 us -> 36.4 us
  starting transfers between devices: 49.2 us -> 37.7 us
    all_to_all x0 -> x1, blocking collectives: none -> 20.5 us  [body(): lax.all_to_all(wide, ('xh', 'y'), 0, 0, tiled=True)]
    all_to_all x2 -> x1, waiting for transfers between devices: 45.9 us -> 32.1 us  [body(): arrived = lax.all_to_all(packed, 'dp', 0, 0, tiled=True)]
    all_to_all x2 -> x1, starting transfers between devices: 35.9 us -> 29.4 us  [body(): arrived = lax.all_to_all(packed, 'dp', 0, 0, tiled=True)]
    ppermute x4 -> x2, starting transfers between devices: 13.3 us -> 8.27 us  [the longest x1 6.07 us: body(): got = lax.ppermute(own, 'co', swap)]
    ppermute x4 -> x2, waiting for transfers between devices: 2.4 us -> 4.33 us  [the longest x1 2.26 us: body(): got = lax.ppermute(own, 'co', swap)]
  transfers between devices with their start and end apart: 6 -> 3, of which waited for: 5 -> 3; matrix products, arithmetic and copies ran while one was open for 1% -> 0% of each run, Pallas kernels for 1% -> 0%
where the time goes in v5:
time: 103 us; the launch traced here: 102 us
  starting transfers between devices  37.7 us (37%)
  waiting for transfers between devices  36.4 us (35%)
  blocking collectives  20.5 us (20%)
  Pallas kernels  5.4 us (5%)
    all_to_all x1, waiting for transfers between devices, body(): arrived = lax.all_to_all(packed, 'dp', 0, 0, tiled=True)  32.1 us
    all_to_all x1, starting transfers between devices, body(): arrived = lax.all_to_all(packed, 'dp', 0, 0, tiled=True)  29.4 us
    all_to_all x1, blocking collectives, body(): lax.all_to_all(wide, ('xh', 'y'), 0, 0, tiled=True)  20.5 us
    ppermute x1, starting transfers between devices, body(): got = lax.ppermute(own, 'co', swap)  6.07 us
    pallas_call x1, Pallas kernels, attend(): pl.pallas_call(attend_kernel, out_shape=(jax.ShapeDtypeStruct((rows, widt...  3.27 us
    ppermute x1, waiting for transfers between devices, body(): got = lax.ppermute(own, 'co', swap)  2.26 us
    ppermute x1, starting transfers between devices, body(): value_out = partial_value + lax.ppermute(partial_value, 'tp', swap)  2.2 us
    ppermute x1, waiting for transfers between devices, body(): value_out = partial_value + lax.ppermute(partial_value, 'tp', swap)  2.06 us
  transfers between devices with their start and end apart: 3, of which 3 were waited for; matrix products, arithmetic and copies ran while one was open for 0% of the time, Pallas kernels for 0%

profile of v5, /device:TPU:1, one launch (start us, length us, event | category | flops | bytes accessed | tf_op | source)
XLA Modules:
  0.0 102.0 jit_solution(3315574776375920761)
XLA Ops:
  0.6 1.9 %shard_map.86 = bf16[32,4,640]{2,1,0:T(4,128)(2,1)} custom-call(bf16[64,2,256]{2,1,0:T(2,128)(2,1)} %bitcast.23, s32[1,64]{1,0:T(1,128)} %bitcast.24, s32[1,64]{1,0:T(1,128)} %bitcast.25), custom_call_target="tpu_custom_call" | custom-call | tf_op jit(solution)/shard_map/pallas_call | solution.py:42
  2.5 0.0 copy-start
  2.5 0.0 copy-start.1
  2.5 29.4 %all-to-all-start = ((bf16[32,4,640]{2,1,0:T(4,128)(2,1)}), bf16[32,4,640]{2,1,0:T(4,128)(2,1)S(1)}, u32[]{:S(2)}, u32[]{:S(2)}) async-start(bf16[32,4,640]{2,1,0:T(4,128)(2,1)} %shard_map.86), calls=%async_computation | async-start | bytes 327680 | tf_op jit(solution)/shard_map/all_to_all | solution.py:172
  31.9 0.0 copy-start.3
  31.9 0.7 copy-done.3
  32.6 0.1 pad_add_fusion.place_ref
  32.7 32.1 %all-to-all-done.arrived_ref = bf16[32,4,640]{2,1,0:T(4,128)(2,1)S(1)} async-done(((bf16[32,4,640]{2,1,0:T(4,128)(2,1)}), bf16[32,4,640]{2,1,0:T(4,128)(2,1)S(1)}, u32[]{:S(2)}, u32[]{:S(2)}) %all-to-all-start) | async-done | bytes 163872 | tf_op jit(solution)/shard_map/all_to_all | solution.py:172
  64.8 0.0 copy-done
  64.8 0.0 copy-done.1
  64.8 0.3 shard_map.87
  65.1 0.0 copy-start.2
  65.1 20.5 %all_to_all.10 = bf16[8,128,512]{2,1,0:T(8,128)(2,1)S(1)} all-to-all(bf16[8,128,512]{2,1,0:T(8,128)(2,1)S(1)} %shard_map.87), channel_id=1, replica_groups=mesh['dp'=32,'xh'=2,'y'=4,'co'=2,'tp'=2] {'xh','y'}, dimensions={0} | all-to-all | bytes 2097152 | tf_op jit(solution)/shard_map/all_to_all | solution.py:181
  85.6 6.1 %collective-permute-start = (bf16[1024,512]{1,0:T(8,128)(2,1)S(1)}, bf16[1024,512]{1,0:T(8,128)(2,1)S(1)}, u32[]{:S(2)}, u32[]{:S(2)}) collective-permute-start(bf16[1024,512]{1,0:T(8,128)(2,1)S(1)} %bitcast.17), channel_id=1, source_target_pairs={{0,2},{2,0},{1,3},{3,1},{4,6},{6,4},{5,7},{7,5},{8,10},{10,8},{9,1... | collective-permute-start | bytes 3145736 | tf_op jit(solution)/shard_map/ppermute | solution.py:182
  91.7 2.3 %collective-permute-done.got_ref = bf16[1024,512]{1,0:T(8,128)(2,1)S(1)} collective-permute-done((bf16[1024,512]{1,0:T(8,128)(2,1)S(1)}, bf16[1024,512]{1,0:T(8,128)(2,1)S(1)}, u32[]{:S(2)}, u32[]{:S(2)}) %collective-permute-start) | collective-permute-done | bytes 1048608 | tf_op jit(solution)/shard_map/ppermute | solution.py:182
  94.0 0.0 copy-done.2
  94.0 3.3 %shard_map.88 = (bf16[128,2048]{1,0:T(8,128)(2,1)}, f32[8,128]{1,0:T(8,128)S(1)}) custom-call(s32[2]{0:T(128)S(1)} %pad_add_fusion.place_ref, bf16[128,2048]{1,0:T(8,128)(2,1)S(1)} %bitcast.22, bf16[1024,512]{1,0:T(8,128)(2,1)S(1)} %bitcast.18, bf16[1024,512]{1,0:T(8,128)(2,1)S(1)} %collective-permute-done.got_ref, f32[1,2048]{1,0:T(1,128)S(1)} %bitcast.21), custom_call_target="tpu_custom_call" | custom-call | flops 2147483648 | bytes 1048576 | tf_op jit(solution)/shard_map/pallas_call | solution.py:141
  97.2 2.2 %collective-permute-start.1 = (f32[128]{0:T(128)S(1)}, f32[128]{0:T(128)S(1)}, u32[]{:S(2)}, u32[]{:S(2)}) collective-permute-start(f32[128]{0:T(128)S(1)} %slice_bitcast_fusion), channel_id=1, source_target_pairs={{0,1},{1,0},{2,3},{3,2},{4,5},{5,4},{6,7},{7,6},{8,9},{9,8},{10,11... | collective-permute-start | bytes 1544 | tf_op jit(solution)/shard_map/ppermute | solution.py:185
  99.4 2.1 %collective-permute-done.1 = f32[128]{0:T(128)S(1)} collective-permute-done((f32[128]{0:T(128)S(1)}, f32[128]{0:T(128)S(1)}, u32[]{:S(2)}, u32[]{:S(2)}) %collective-permute-start.1) | collective-permute-done | bytes 544 | tf_op jit(solution)/shard_map/ppermute | solution.py:185
  101.5 0.5 add_bitcast_fusion
  (2 shorter events, 0.0 us)
Async XLA Ops:
  2.5 62.3 %copy-start = (bf16[1,128,256]{2,1,0:T(8,128)(2,1)S(1)}, bf16[1,128,256]{2,1,0:T(8,128)(2,1)}, u32[]{:S(2)}) copy-start(bf16[1,128,256]{2,1,0:T(8,128)(2,1)} %param.8) | copy-start | bytes 196612
  2.5 62.3 %copy-start.1 = (bf16[1,128,256]{2,1,0:T(8,128)(2,1)S(1)}, bf16[1,128,256]{2,1,0:T(8,128)(2,1)}, u32[]{:S(2)}) copy-start(bf16[1,128,256]{2,1,0:T(8,128)(2,1)} %param.9) | copy-start | bytes 196612
  2.5 62.3 %all-to-all-start = ((bf16[32,4,640]{2,1,0:T(4,128)(2,1)}), bf16[32,4,640]{2,1,0:T(4,128)(2,1)S(1)}, u32[]{:S(2)}, u32[]{:S(2)}) async-start(bf16[32,4,640]{2,1,0:T(4,128)(2,1)} %shard_map.86), calls=%async_computation | async-start | bytes 327680 | tf_op jit(solution)/shard_map/all_to_all | solution.py:172
  31.9 0.7 copy-start.3
  65.1 28.9 %copy-start.2 = (bf16[1,128,2048]{2,1,0:T(8,128)(2,1)S(1)}, bf16[1,128,2048]{2,1,0:T(8,128)(2,1)}, u32[]{:S(2)}) copy-start(bf16[1,128,2048]{2,1,0:T(8,128)(2,1)} %param.7) | copy-start | bytes 1572868
  85.6 8.3 %collective-permute-start = (bf16[1024,512]{1,0:T(8,128)(2,1)S(1)}, bf16[1024,512]{1,0:T(8,128)(2,1)S(1)}, u32[]{:S(2)}, u32[]{:S(2)}) collective-permute-start(bf16[1024,512]{1,0:T(8,128)(2,1)S(1)} %bitcast.17), channel_id=1, source_target_pairs={{0,2},{2,0},{1,3},{3,1},{4,6},{6,4},{5,7},{7,5},{8,10},{10,8},{9,1... | collective-permute-start | bytes 3145736 | tf_op jit(solution)/shard_map/ppermute | solution.py:182
  97.2 4.3 %collective-permute-start.1 = (f32[128]{0:T(128)S(1)}, f32[128]{0:T(128)S(1)}, u32[]{:S(2)}, u32[]{:S(2)}) collective-permute-start(f32[128]{0:T(128)S(1)} %slice_bitcast_fusion), channel_id=1, source_target_pairs={{0,1},{1,0},{2,3},{3,2},{4,5},{5,4},{6,7},{7,6},{8,9},{9,8},{10,11... | collective-permute-start | bytes 1544 | tf_op jit(solution)/shard_map/ppermute | solution.py:185

commit v6 on v5

--- a/solution.py
+++ b/solution.py
@@ -9,6 +9,7 @@
 HD = 128
 CAP = 4
 CHUNK = 256
+STACK = 2
 LOG2E = 1.4426950408889634
 
 
@@ -77,48 +78,56 @@
     )(arrived, keys_text, values_text)
 
 
-def attend_kernel(place_ref, queries_ref, own_ref, got_ref, head_ref, out_ref, value_ref):
+def attend_kernel(queries_ref, own_ref, got_ref, head_ref, out_ref, value_ref):
     rows, width = queries_ref.shape
     length = own_ref.shape[0]
     groups = own_ref.shape[1] // (2 * HD)
     heads = width // HD
     factor = HD ** (-0.5) * LOG2E
-    chip, core = place_ref[0], place_ref[1]
+    chip = lax.axis_index("xh") * lax.axis_size("y") + lax.axis_index("y")
+    core = lax.axis_index("co")
 
     def attend_first(count):
         whole = count - CHUNK
-        key = lax.broadcasted_iota(jnp.int32, (rows, CHUNK), 1) + whole
-        query = lax.broadcasted_iota(jnp.int32, (rows, CHUNK), 0)
+        key = lax.broadcasted_iota(jnp.int32, (STACK * rows, CHUNK), 1) + whole
+        query = lax.broadcasted_iota(jnp.int32, (STACK * rows, CHUNK), 0) % rows
         block, spot = key // rows, key % rows
         own_allowed = (block < chip) | ((block == chip) & (spot <= query))
         got_allowed = block < chip + core
         value = jnp.zeros((rows, HD), jnp.float32)
-        for h in range(heads):
-            g = h // (heads // groups)
-            queries = queries_ref[:, h * HD : (h + 1) * HD]
-            scores = []
-            for ref, allowed in ((own_ref, own_allowed), (got_ref, got_allowed)):
-                part = lax.dot_general(
-                    queries,
-                    ref[:count, g * HD : (g + 1) * HD],
-                    (((1,), (1,)), ((), ())),
-                    preferred_element_type=jnp.float32,
-                )
-                if whole:
-                    scores.append(part[:, :whole])
-                scores.append(jnp.where(allowed, part[:, whole:], -1e30))
-            scores = jnp.concatenate(scores, axis=1)
-            top = jnp.max(scores, axis=1, keepdims=True)
-            weights = jnp.exp2((scores - top) * factor).astype(jnp.bfloat16)
+        for g in range(groups):
             lower = (groups + g) * HD
             values = jnp.concatenate(
                 [own_ref[:count, lower : lower + HD], got_ref[:count, lower : lower + HD]], axis=0
             )
             values = jnp.concatenate([values, jnp.ones((2 * count, HD), jnp.bfloat16)], axis=1)
-            mixed = jnp.dot(weights, values, preferred_element_type=jnp.float32)
-            out = (mixed[:, :HD] / mixed[:, HD:]).astype(jnp.bfloat16)
-            out_ref[:, h * HD : (h + 1) * HD] = out
-            value = value + out.astype(jnp.float32) * head_ref[:, h * HD : (h + 1) * HD]
+            for first in range(g * heads // groups, (g + 1) * heads // groups, STACK):
+                stack = range(first, first + STACK)
+                queries = jnp.concatenate(
+                    [queries_ref[:, h * HD : (h + 1) * HD] for h in stack], axis=0
+                )
+                scores = []
+                for ref, allowed in ((own_ref, own_allowed), (got_ref, got_allowed)):
+                    part = lax.dot_general(
+                        queries,
+                        ref[:count, g * HD : (g + 1) * HD],
+                        (((1,), (1,)), ((), ())),
+                        preferred_element_type=jnp.float32,
+                    )
+                    if whole:
+                        scores.append(part[:, :whole])
+                    scores.append(jnp.where(allowed, part[:, whole:], -1e30))
+                scores = jnp.concatenate(scores, axis=1)
+                top = jnp.max(scores, axis=1, keepdims=True)
+                weights = jnp.exp2((scores - top) * factor).astype(jnp.bfloat16)
+                mixed = jnp.dot(weights, values, preferred_element_type=jnp.float32)
+                out = (mixed[:, :HD] / mixed[:, HD:]).astype(jnp.bfloat16)
+                for i, h in enumerate(stack):
+                    part = out[i * rows : (i + 1) * rows]
+                    out_ref[:, h * HD : (h + 1) * HD] = part
+                    value = value + part.astype(jnp.float32) * head_ref[
+                        :, h * HD : (h + 1) * HD
+                    ].astype(jnp.float32)
         value_ref[...] = lax.dot_general(
             jnp.ones((8, HD), jnp.float32),
             value,
@@ -134,7 +143,7 @@
             attend_first((i + 1) * CHUNK)
 
 
-def attend(place, queries, own, got, head):
+def attend(queries, own, got, head):
     rows, width = queries.shape
     vmem = pl.BlockSpec(memory_space=pltpu.VMEM)
     pairs = 2 * rows * width * own.shape[0]
@@ -144,21 +153,19 @@
             jax.ShapeDtypeStruct((rows, width), jnp.bfloat16),
             jax.ShapeDtypeStruct((8, rows), jnp.float32),
         ),
-        in_specs=[pl.BlockSpec(memory_space=pltpu.SMEM), vmem, vmem, vmem, vmem],
+        in_specs=[vmem, vmem, vmem, vmem],
         out_specs=(vmem, vmem),
         compiler_params=pltpu.CompilerParams(vmem_limit_bytes=40 * 2**20),
         cost_estimate=pl.CostEstimate(
             flops=4 * pairs, bytes_accessed=4 * rows * width, transcendentals=pairs // HD
         ),
-    )(place, queries, own, got, head)
+    )(queries, own, got, head)
 
 
 def body(queries, keys_text, values_text, patch_rows, patch_owner, patch_place, value_head):
     rows = queries.shape[1]
     dp_count = lax.axis_size("dp")
     chip_count = lax.axis_size("xh") * lax.axis_size("y")
-    core = lax.axis_index("co")
-    chip = lax.axis_index("xh") * lax.axis_size("y") + lax.axis_index("y")
     swap = [(0, 1), (1, 0)]
     count = patch_rows.shape[2]
     width = 2 * keys_text.shape[2]
@@ -170,20 +177,11 @@
         dp_count,
     )
     arrived = lax.all_to_all(packed, "dp", 0, 0, tiled=True)
-    own_queries = queries[0]
-    head = value_head[None].astype(jnp.float32)
-    place = jnp.stack([chip, core])
-    arrived, own_queries, head, place, keys_text, values_text = lax.optimization_barrier(
-        (arrived, own_queries, head, place, keys_text, values_text)
-    )
     wide = merge(arrived, keys_text[0], values_text[0], chip_count)
-    wide, own_queries, head, place = lax.optimization_barrier((wide, own_queries, head, place))
     own = lax.all_to_all(wide, ("xh", "y"), 0, 0, tiled=True).reshape(chip_count * rows, width)
     got = lax.ppermute(own, "co", swap)
-    attention, value = attend(place, own_queries, own, got, head)
-    partial_value = value[0]
-    value_out = partial_value + lax.ppermute(partial_value, "tp", swap)
-    return attention[None], value_out[None]
+    attention, value = attend(queries[0], own, got, value_head[None])
+    return attention[None], lax.psum(value[:1], "tp")
 
 
 def solution(mesh):

time: 103 us -> 101 us (0.981)
  blocking collectives: 20.5 us -> 87.1 us
  waiting for transfers between devices: 36.4 us -> 2.24 us
  starting transfers between devices: 37.7 us -> 6.07 us
    all_to_all x0 -> x1, blocking collectives: none -> 62.3 us  [body(): arrived = lax.all_to_all(packed, 'dp', 0, 0, tiled=True)]
    all_to_all x1 -> x0, waiting for transfers between devices: 32.1 us -> none  [body(): arrived = lax.all_to_all(packed, 'dp', 0, 0, tiled=True)]
    all_to_all x1 -> x0, starting transfers between devices: 29.4 us -> none  [body(): arrived = lax.all_to_all(packed, 'dp', 0, 0, tiled=True)]
    psum x0 -> x1, blocking collectives: none -> 4.27 us  [body(): return (attention[None], lax.psum(value[:1], 'tp'))]
    ppermute x1 -> x0, starting transfers between devices: 2.2 us -> none  [body(): value_out = partial_value + lax.ppermute(partial_value, 'tp', swap)]
    ppermute x1 -> x0, waiting for transfers between devices: 2.06 us -> none  [body(): value_out = partial_value + lax.ppermute(partial_value, 'tp', swap)]
  transfers between devices with their start and end apart: 3 -> 1, of which waited for: 3 -> 1; matrix products, arithmetic and copies ran while one was open for 0% -> 0% of each run, Pallas kernels for 0% -> 0%
where the time goes in v6:
time: 101 us
  blocking collectives  87.1 us (86%)
  starting transfers between devices  6.07 us (6%)
  Pallas kernels  4.85 us (5%)
  waiting for transfers between devices  2.24 us (2%)
    all_to_all x1, blocking collectives, body(): arrived = lax.all_to_all(packed, 'dp', 0, 0, tiled=True)  62.3 us
    all_to_all x1, blocking collectives, body(): lax.all_to_all(wide, ('xh', 'y'), 0, 0, tiled=True)  20.5 us
    ppermute x1, starting transfers between devices, body(): got = lax.ppermute(own, 'co', swap)  6.07 us
    psum x1, blocking collectives, body(): return (attention[None], lax.psum(value[:1], 'tp'))  4.27 us
    pallas_call x1, Pallas kernels, attend(): pl.pallas_call(attend_kernel, out_shape=(jax.ShapeDtypeStruct((rows, widt...  2.72 us
    ppermute x1, waiting for transfers between devices, body(): got = lax.ppermute(own, 'co', swap)  2.24 us
  transfers between devices with their start and end apart: 1, of which 1 were waited for; matrix products, arithmetic and copies ran while one was open for 0% of the time, Pallas kernels for 0%

profile of v6, /device:TPU:1, one launch (start us, length us, event | category | flops | bytes accessed | tf_op | source)
XLA Modules:
  0.0 101.0 jit_solution(7686766315090080494)
XLA Ops:
  0.6 1.9 %shard_map.86 = bf16[32,4,640]{2,1,0:T(4,128)(2,1)} custom-call(bf16[64,2,256]{2,1,0:T(2,128)(2,1)} %bitcast.13, s32[1,64]{1,0:T(1,128)} %bitcast.14, s32[1,64]{1,0:T(1,128)} %bitcast.15), custom_call_target="tpu_custom_call" | custom-call | tf_op jit(solution)/shard_map/pallas_call | solution.py:43
  2.5 0.0 copy-start
  2.5 0.0 copy-start.1
  2.5 62.3 %all_to_all.10.arrived_ref = bf16[32,4,640]{2,1,0:T(4,128)(2,1)S(1)} all-to-all(bf16[32,4,640]{2,1,0:T(4,128)(2,1)} %shard_map.86), channel_id=1, replica_groups=mesh['dp'=32,'xh'=2,'y'=4,'co'=2,'tp'=2] {'dp'}, dimensions={0} | all-to-all | bytes 327680 | tf_op jit(solution)/shard_map/all_to_all | solution.py:179
  64.8 0.0 copy-done
  64.8 0.0 copy-done.1
  64.8 0.3 shard_map.87
  65.1 0.0 copy-start.3
  65.1 0.0 copy-start.2
  65.1 20.5 %all_to_all.11 = bf16[8,128,512]{2,1,0:T(8,128)(2,1)S(1)} all-to-all(bf16[8,128,512]{2,1,0:T(8,128)(2,1)S(1)} %shard_map.87), channel_id=1, replica_groups=mesh['dp'=32,'xh'=2,'y'=4,'co'=2,'tp'=2] {'xh','y'}, dimensions={0} | all-to-all | bytes 2097152 | tf_op jit(solution)/shard_map/all_to_all | solution.py:181
  85.6 6.1 %collective-permute-start = (bf16[1024,512]{1,0:T(8,128)(2,1)S(1)}, bf16[1024,512]{1,0:T(8,128)(2,1)S(1)}, u32[]{:S(2)}, u32[]{:S(2)}) collective-permute-start(bf16[1024,512]{1,0:T(8,128)(2,1)S(1)} %bitcast.8), channel_id=1, source_target_pairs={{0,2},{2,0},{1,3},{3,1},{4,6},{6,4},{5,7},{7,5},{8,10},{10,8},{9,1... | collective-permute-start | bytes 3145736 | tf_op jit(solution)/shard_map/ppermute | solution.py:182
  91.7 0.0 copy-done.3
  91.7 2.2 %collective-permute-done.got_ref = bf16[1024,512]{1,0:T(8,128)(2,1)S(1)} collective-permute-done((bf16[1024,512]{1,0:T(8,128)(2,1)S(1)}, bf16[1024,512]{1,0:T(8,128)(2,1)S(1)}, u32[]{:S(2)}, u32[]{:S(2)}) %collective-permute-start) | collective-permute-done | bytes 1048608 | tf_op jit(solution)/shard_map/ppermute | solution.py:182
  94.0 0.0 copy-done.2
  94.0 2.7 %shard_map.88 = (bf16[128,2048]{1,0:T(8,128)(2,1)}, f32[8,128]{1,0:T(8,128)S(1)}) custom-call(bf16[128,2048]{1,0:T(8,128)(2,1)S(1)} %bitcast.12, bf16[1024,512]{1,0:T(8,128)(2,1)S(1)} %bitcast.9, bf16[1024,512]{1,0:T(8,128)(2,1)S(1)} %collective-permute-done.got_ref, bf16[1,2048]{1,0:T(2,128)(2,1)S(1)} %broadcast_in_dim.6.head_ref), custom_call_target="tpu_custom_call" | custom-call | flops 2147483648 | bytes 1048576 | tf_op jit(solution)/shard_map/pallas_call | solution.py:150
  96.7 4.3 %psum.7 = f32[1,128]{1,0:T(1,128)} all-reduce(f32[1,128]{1,0:T(1,128)S(1)} %slice.3), channel_id=1, replica_groups=mesh['dp'=32,'xh'=2,'y'=4,'co'=2,'tp'=2] {'tp'}, use_global_device_ids=true, to_apply=%region_0.0 | all-reduce | flops 128 | bytes 1024 | tf_op jit(solution)/shard_map/psum | solution.py:184
  (2 shorter events, 0.0 us)
Async XLA Ops:
  2.5 62.3 %copy-start = (bf16[1,128,256]{2,1,0:T(8,128)(2,1)S(1)}, bf16[1,128,256]{2,1,0:T(8,128)(2,1)}, u32[]{:S(2)}) copy-start(bf16[1,128,256]{2,1,0:T(8,128)(2,1)} %param.8) | copy-start | bytes 196612
  2.5 62.3 %copy-start.1 = (bf16[1,128,256]{2,1,0:T(8,128)(2,1)S(1)}, bf16[1,128,256]{2,1,0:T(8,128)(2,1)}, u32[]{:S(2)}) copy-start(bf16[1,128,256]{2,1,0:T(8,128)(2,1)} %param.9) | copy-start | bytes 196612
  65.1 26.6 %copy-start.3 = (bf16[2048]{0:T(1024)(128)(2,1)S(1)}, bf16[2048]{0:T(1024)(128)(2,1)}, u32[]{:S(2)}) copy-start(bf16[2048]{0:T(1024)(128)(2,1)} %param.13) | copy-start | bytes 12292
  65.1 28.9 %copy-start.2 = (bf16[1,128,2048]{2,1,0:T(8,128)(2,1)S(1)}, bf16[1,128,2048]{2,1,0:T(8,128)(2,1)}, u32[]{:S(2)}) copy-start(bf16[1,128,2048]{2,1,0:T(8,128)(2,1)} %param.7) | copy-start | bytes 1572868
  85.6 8.3 %collective-permute-start = (bf16[1024,512]{1,0:T(8,128)(2,1)S(1)}, bf16[1024,512]{1,0:T(8,128)(2,1)S(1)}, u32[]{:S(2)}, u32[]{:S(2)}) collective-permute-start(bf16[1024,512]{1,0:T(8,128)(2,1)S(1)} %bitcast.8), channel_id=1, source_target_pairs={{0,2},{2,0},{1,3},{3,1},{4,6},{6,4},{5,7},{7,5},{8,10},{10,8},{9,1... | collective-permute-start | bytes 3145736 | tf_op jit(solution)/shard_map/ppermute | solution.py:182
